TPU v7x, 32 devices: a whole 2x2x4 slice. The times are simulated.
32 devices in a mesh: depth: 8 (over z, y), gx: 2 (over core), gy: 2 (over x).
Axes of the slice: x: 2, y: 2, z: 4, core: 2. Of those that a mesh axis runs over, the one named last changes fastest.
Arguments:
- slowness: float32 [16, 32, 512], P('depth', 'gx', 'gy'), may hold values from 0.5 to 1.5
- air_mask: int32 [16, 32, 512], P('depth', 'gx', 'gy'), may hold values from 0 to 1, as said below
- reflector: int32 [32, 512], P('gx', 'gy'), may hold values from 4 to 15
- shot_cells: int32 [8, 2], replicated, may hold values from 0 to 31
- receiver_mask: int32 [8, 32, 512], P(None, 'gx', 'gy'), may hold values 0 or 1
- residual: float32 [8, 32, 512], P(None, 'gx', 'gy'), may hold values from -6 to 6
Outputs:
- gradient: float32 [16, 32, 512], P('depth', 'gx', 'gy')
Inputs may be any that keep to these rules, and one draw needn't show every extreme that they name: `air_mask`: each lateral column is air in a top run of 0 to 2 cells and earth below; some column has exactly 2 air cells.
All inputs are finite; a program needn't handle non-finite values. No bound on the sum of `receiver_mask` on one device may be relied on, other than what follows from the above.
Results may differ from a plain program's by a relative error of at most 0.0003.
Values sent between devices are 32-bit elements; how exact they have to be, the bound alone decides.
A program may use at most 64 MiB of HBM per device.

v0:
```python
import math

import jax
import jax.numpy as jnp
from jax import lax
from jax.sharding import PartitionSpec as P

SOFTMIN_TEMPER = 0.5
SURF = 0.7
AIR_SLOW = 2.5
STEP_PENALTY = 10000.0
STENCIL_SHIFTS = [
    (first_term, second_term) for first_term in (-1, 0, 1) for second_term in (-1, 0, 1)
]


def padded(cells, sides, width):
    for axis, dim in sides:
        count = lax.axis_size(axis)
        ends = count - 1
        head = lax.slice_in_dim(cells, 0, width, axis=dim)
        tail = lax.slice_in_dim(cells, cells.shape[dim] - width, cells.shape[dim], axis=dim)
        cells = jnp.concatenate(
            [
                lax.ppermute(tail, axis, [(i, (i + 1) % count) for i in range(ends)]),
                cells,
                lax.ppermute(head, axis, [((i + 1) % count, i) for i in range(ends)]),
            ],
            axis=dim,
        )
    return cells


def passed_along(value, axis, steps):
    count = lax.axis_size(axis)
    initial, last = (max(0, -steps), min(count, count - steps))
    return lax.ppermute(value, axis, [(source, source + steps) for source in range(initial, last)])


def soft_front(candidate_times):
    lowest = candidate_times[0]
    for cand in candidate_times[1:]:
        lowest = jnp.minimum(lowest, cand)
    total = jnp.exp(-(candidate_times[0] - lowest) / SOFTMIN_TEMPER)
    for cand in candidate_times[1:]:
        total = total + jnp.exp(-(cand - lowest) / SOFTMIN_TEMPER)
    return lowest - SOFTMIN_TEMPER * jnp.log(total)


def local(slowness, air_mask, reflector, shot_cells, receiver_mask, residual):
    depth_count = lax.axis_size("depth")
    depth_pos = lax.axis_index("depth")
    cz, shift_along_x, shift_along_y = slowness.shape
    shots = shot_cells.shape[0]
    nx_total = shift_along_x * lax.axis_size("gx")
    ny_total = shift_along_y * lax.axis_size("gy")
    xpos = lax.axis_index("gx") * shift_along_x + jnp.arange(shift_along_x, dtype=jnp.int32)
    ypos = lax.axis_index("gy") * shift_along_y + jnp.arange(shift_along_y, dtype=jnp.int32)
    zpos = depth_pos * cz + jnp.arange(cz, dtype=jnp.int32)
    earth = air_mask == 0
    speed = jnp.where(air_mask == 1, jnp.float32(AIR_SLOW), slowness)
    shot_x = shot_cells[:, 0].astype(jnp.float32)
    shot_y = shot_cells[:, 1].astype(jnp.float32)
    surface = SURF * jnp.sqrt(
        (xpos.astype(jnp.float32)[None, :, None] - shot_x[:, None, None]) ** 2
        + (ypos.astype(jnp.float32)[None, None, :] - shot_y[:, None, None]) ** 2
    )
    penalty_terms = []
    span_lengths = []
    for first_term, second_term in STENCIL_SHIFTS:
        valid_mask = ((xpos + first_term >= 0) & (xpos + first_term < nx_total))[:, None] & (
            (ypos + second_term >= 0) & (ypos + second_term < ny_total)
        )[None, :]
        penalty_terms.append(jnp.where(valid_mask, jnp.float32(0.0), jnp.float32(STEP_PENALTY)))
        span_lengths.append(math.sqrt(1.0 + first_term * first_term + second_term * second_term))

    def sweep_plane(prior_layer, depth_layer):
        padded_layer = padded(prior_layer, (("gx", 1), ("gy", 2)), 1)
        candidate_times = [
            padded_layer[
                :,
                1 + first_term : 1 + first_term + shift_along_x,
                1 + second_term : 1 + second_term + shift_along_y,
            ]
            + depth_layer * span_lengths[stencil_index]
            + penalty_terms[stencil_index]
            for stencil_index, (first_term, second_term) in enumerate(STENCIL_SHIFTS)
        ]
        nxt = soft_front(candidate_times)
        return (nxt, nxt)

    def make_adjoint(source_block, count):

        def adjoint_plane(back, inputs):
            depth_layer, hit, previous_times, current_layer = inputs
            lam = source_block * hit[None] + back
            stacked = jnp.concatenate([lam, current_layer, previous_times, depth_layer[None]], 0)
            padded_layer = padded(stacked, (("gx", 1), ("gy", 2)), 1)
            lam_pad = padded_layer[:count]
            cur_pad = padded_layer[count : 2 * count]
            prev_pad = padded_layer[2 * count : 3 * count]
            layer_pad = padded_layer[3 * count]
            weight_sum = jnp.zeros_like(lam)
            back_new = jnp.zeros_like(lam)
            for stencil_index, (first_term, second_term) in enumerate(STENCIL_SHIFTS):
                lateral_value = prev_pad[
                    :,
                    1 + first_term : 1 + first_term + shift_along_x,
                    1 + second_term : 1 + second_term + shift_along_y,
                ]
                softmin_weight = jnp.exp(
                    -(
                        lateral_value
                        + depth_layer * span_lengths[stencil_index]
                        + penalty_terms[stencil_index]
                        - current_layer
                    )
                    / SOFTMIN_TEMPER
                )
                weight_sum = weight_sum + softmin_weight * span_lengths[stencil_index]
                lam_from = lam_pad[
                    :,
                    1 - first_term : 1 - first_term + shift_along_x,
                    1 - second_term : 1 - second_term + shift_along_y,
                ]
                cur_from = cur_pad[
                    :,
                    1 - first_term : 1 - first_term + shift_along_x,
                    1 - second_term : 1 - second_term + shift_along_y,
                ]
                layer_from = layer_pad[
                    1 - first_term : 1 - first_term + shift_along_x,
                    1 - second_term : 1 - second_term + shift_along_y,
                ]
                prob_from = jnp.exp(
                    -(previous_times + layer_from * span_lengths[stencil_index] - cur_from)
                    / SOFTMIN_TEMPER
                )
                back_new = back_new + lam_from * prob_from
            return (back_new, jnp.sum(lam * weight_sum, axis=0))

        return adjoint_plane

    source_all = jnp.where(receiver_mask == 1, residual, jnp.float32(0.0))
    blocks = 1
    width = shots // blocks
    rounds = depth_count + blocks - 1

    def forward_round(step, carry):
        incoming, store = carry
        group = step - depth_pos
        valid_mask = (group >= 0) & (group < blocks)
        top = jnp.where(depth_pos == 0, surface, incoming)
        last, planes = lax.scan(sweep_plane, top, speed)
        block = jnp.concatenate([top[None], planes], 0)
        old = store
        store = jnp.where(valid_mask, block, old)
        incoming = passed_along(last, "depth", 1)
        return (incoming, store)

    store = jnp.zeros((cz + 1, shots, shift_along_x, shift_along_y), jnp.float32)
    incoming = jnp.zeros((width, shift_along_x, shift_along_y), jnp.float32)
    incoming, store = lax.fori_loop(0, rounds, forward_round, (incoming, store))
    hits = (zpos[:, None, None] == reflector[None]).astype(jnp.float32)

    def adjoint_round(step, carry):
        incoming_back, grad_sum = carry
        group = step - (depth_count - 1 - depth_pos)
        valid_mask = (group >= 0) & (group < blocks)
        back_top, grads = lax.scan(
            make_adjoint(source_all, width),
            incoming_back,
            (speed, hits, store[:-1], store[1:]),
            reverse=True,
        )
        grad_sum = grad_sum + jnp.where(valid_mask, grads, jnp.float32(0.0))
        incoming_back = passed_along(back_top, "depth", -1)
        return (incoming_back, grad_sum)

    start_back = jnp.zeros((width, shift_along_x, shift_along_y), jnp.float32)
    grad_total = jnp.zeros((cz, shift_along_x, shift_along_y), jnp.float32)
    start_back, grad_total = lax.fori_loop(0, rounds, adjoint_round, (start_back, grad_total))
    colsum = jnp.sum(source_all, axis=0)
    below = zpos[:, None, None] <= reflector[None]
    raw = jnp.where(earth, grad_total, jnp.float32(0.0)) + jnp.where(
        earth & below, colsum[None], jnp.float32(0.0)
    )
    padded_layer = padded(raw, (("gx", 1), ("gy", 2)), 1)
    beside_all = jnp.zeros_like(raw)
    for first_term, second_term in STENCIL_SHIFTS:
        if first_term != 0 or second_term != 0:
            beside_all = (
                beside_all
                + padded_layer[
                    :,
                    1 + first_term : 1 + first_term + shift_along_x,
                    1 + second_term : 1 + second_term + shift_along_y,
                ]
            )
    return 0.5 * raw + 0.0625 * beside_all


def solution(mesh):
    in_specs = (
        P("depth", "gx", "gy"),
        P("depth", "gx", "gy"),
        P("gx", "gy"),
        P(),
        P(None, "gx", "gy"),
        P(None, "gx", "gy"),
    )
    out_specs = P("depth", "gx", "gy")
    return jax.shard_map(local, mesh=mesh, in_specs=in_specs, out_specs=out_specs, check_vma=False)
```

profile of v0, /device:TPU:0, one launch (start us, length us, event | category | flops | bytes accessed | tf_op | source)
XLA Modules:
  0.0 695.7 jit_solution(8238866544487550362)
XLA Ops:
  2.7 291.4 %while.130 = (s32[]{:T(128)}, f32[8,16,256]{2,1,0:T(8,128)S(1)}, f32[3,8,16,256]{3,2,1,0:T(8,128)S(1)}, pred[]{:T(512)}, f32[2,16,256]{2,1,0:T(8,128)S(1)}, /*in...) while((s32[]{:T(128)}, f32[8,16,256]{2,1,0:T(8,128)S(1)}, ...), condition=%wide.region_3.4_spmd.clone.clone.clone, body=%wide.region_0.3_spmd.clone.clone.clone.sunk | while | flops 2999145 | bytes 5221840 | solution.py:163
  3.0 31.7 %while.133 = (s32[]{:T(128)}, f32[8,16,256]{2,1,0:T(8,128)S(1)}, f32[2,8,16,256]{3,2,1,0:T(8,128)S(1)}, f32[2,16,256]{2,1,0:T(8,128)S(1)}, f32[16,256]{1,0:T(8,1...) while((s32[]{:T(128)}, f32[8,16,256]{2,1,0:T(8,128)S(1)}, ...), condition=%wide.region_2.2_spmd, body=%wide.region_1.1_spmd.sunk | while | flops 2433890 | bytes 2565429 | solution.py:154
  8.3 4.8 collective-permute-start.7
  40.9 28.5 %while.133 = (s32[]{:T(128)}, f32[8,16,256]{2,1,0:T(8,128)S(1)}, f32[2,8,16,256]{3,2,1,0:T(8,128)S(1)}, f32[2,16,256]{2,1,0:T(8,128)S(1)}, f32[16,256]{1,0:T(8,1...) while((s32[]{:T(128)}, f32[8,16,256]{2,1,0:T(8,128)S(1)}, ...), condition=%wide.region_2.2_spmd, body=%wide.region_1.1_spmd.sunk | while | flops 2433890 | bytes 2565429 | solution.py:154
  76.5 28.5 %while.133 = (s32[]{:T(128)}, f32[8,16,256]{2,1,0:T(8,128)S(1)}, f32[2,8,16,256]{3,2,1,0:T(8,128)S(1)}, f32[2,16,256]{2,1,0:T(8,128)S(1)}, f32[16,256]{1,0:T(8,1...) while((s32[]{:T(128)}, f32[8,16,256]{2,1,0:T(8,128)S(1)}, ...), condition=%wide.region_2.2_spmd, body=%wide.region_1.1_spmd.sunk | while | flops 2433890 | bytes 2565429 | solution.py:154
  112.0 28.5 %while.133 = (s32[]{:T(128)}, f32[8,16,256]{2,1,0:T(8,128)S(1)}, f32[2,8,16,256]{3,2,1,0:T(8,128)S(1)}, f32[2,16,256]{2,1,0:T(8,128)S(1)}, f32[16,256]{1,0:T(8,1...) while((s32[]{:T(128)}, f32[8,16,256]{2,1,0:T(8,128)S(1)}, ...), condition=%wide.region_2.2_spmd, body=%wide.region_1.1_spmd.sunk | while | flops 2433890 | bytes 2565429 | solution.py:154
  140.5 5.2 collective-permute-start.9
  148.5 28.5 %while.133 = (s32[]{:T(128)}, f32[8,16,256]{2,1,0:T(8,128)S(1)}, f32[2,8,16,256]{3,2,1,0:T(8,128)S(1)}, f32[2,16,256]{2,1,0:T(8,128)S(1)}, f32[16,256]{1,0:T(8,1...) while((s32[]{:T(128)}, f32[8,16,256]{2,1,0:T(8,128)S(1)}, ...), condition=%wide.region_2.2_spmd, body=%wide.region_1.1_spmd.sunk | while | flops 2433890 | bytes 2565429 | solution.py:154
  177.0 5.3 collective-permute-start.9
  185.0 28.5 %while.133 = (s32[]{:T(128)}, f32[8,16,256]{2,1,0:T(8,128)S(1)}, f32[2,8,16,256]{3,2,1,0:T(8,128)S(1)}, f32[2,16,256]{2,1,0:T(8,128)S(1)}, f32[16,256]{1,0:T(8,1...) while((s32[]{:T(128)}, f32[8,16,256]{2,1,0:T(8,128)S(1)}, ...), condition=%wide.region_2.2_spmd, body=%wide.region_1.1_spmd.sunk | while | flops 2433890 | bytes 2565429 | solution.py:154
  213.4 5.3 collective-permute-start.9
  221.5 28.5 %while.133 = (s32[]{:T(128)}, f32[8,16,256]{2,1,0:T(8,128)S(1)}, f32[2,8,16,256]{3,2,1,0:T(8,128)S(1)}, f32[2,16,256]{2,1,0:T(8,128)S(1)}, f32[16,256]{1,0:T(8,1...) while((s32[]{:T(128)}, f32[8,16,256]{2,1,0:T(8,128)S(1)}, ...), condition=%wide.region_2.2_spmd, body=%wide.region_1.1_spmd.sunk | while | flops 2433890 | bytes 2565429 | solution.py:154
  249.9 5.3 collective-permute-start.9
  257.9 28.5 %while.133 = (s32[]{:T(128)}, f32[8,16,256]{2,1,0:T(8,128)S(1)}, f32[2,8,16,256]{3,2,1,0:T(8,128)S(1)}, f32[2,16,256]{2,1,0:T(8,128)S(1)}, f32[16,256]{1,0:T(8,1...) while((s32[]{:T(128)}, f32[8,16,256]{2,1,0:T(8,128)S(1)}, ...), condition=%wide.region_2.2_spmd, body=%wide.region_1.1_spmd.sunk | while | flops 2433890 | bytes 2565429 | solution.py:154
  286.4 5.3 collective-permute-start.9
  294.9 385.3 %while.132 = (s32[]{:T(128)}, f32[8,16,256]{2,1,0:T(8,128)S(1)}, f32[2,16,256]{2,1,0:T(8,128)S(1)}, f32[3,8,16,256]{3,2,1,0:T(8,128)S(1)}, f32[8,16,256]{2,1,0:T...) while((s32[]{:T(128)}, f32[8,16,256]{2,1,0:T(8,128)S(1)}, ...), condition=%wide.region_8.9_spmd.clone.clone.clone, body=%wide.region_4.8_spmd.clone.clone.clone.sunk | while | flops 6839326 | bytes 10794326 | solution.py:182
  295.1 39.9 %while.134 = (s32[]{:T(128)}, f32[8,16,256]{2,1,0:T(8,128)S(1)}, f32[2,16,256]{2,1,0:T(8,128)S(1)}, f32[2,16,256]{2,1,0:T(8,128)S(1)}, f32[8,16,256]{2,1,0:T(8,1...) while((s32[]{:T(128)}, f32[8,16,256]{2,1,0:T(8,128)S(1)}, ...), condition=%wide.region_7.7_spmd, body=%wide.region_5.6_spmd.sunk | while | flops 6724631 | bytes 8630401 | solution.py:170
  306.6 5.5 collective-permute-done.2
  326.5 5.6 collective-permute-done.2
  336.4 6.9 collective-permute-done.4
  343.6 40.0 %while.134 = (s32[]{:T(128)}, f32[8,16,256]{2,1,0:T(8,128)S(1)}, f32[2,16,256]{2,1,0:T(8,128)S(1)}, f32[2,16,256]{2,1,0:T(8,128)S(1)}, f32[8,16,256]{2,1,0:T(8,1...) while((s32[]{:T(128)}, f32[8,16,256]{2,1,0:T(8,128)S(1)}, ...), condition=%wide.region_7.7_spmd, body=%wide.region_5.6_spmd.sunk | while | flops 6724631 | bytes 8630401 | solution.py:170
  355.1 5.6 collective-permute-done.2
  375.1 5.6 collective-permute-done.2
  384.9 6.9 collective-permute-done.4
  392.1 40.0 %while.134 = (s32[]{:T(128)}, f32[8,16,256]{2,1,0:T(8,128)S(1)}, f32[2,16,256]{2,1,0:T(8,128)S(1)}, f32[2,16,256]{2,1,0:T(8,128)S(1)}, f32[8,16,256]{2,1,0:T(8,1...) while((s32[]{:T(128)}, f32[8,16,256]{2,1,0:T(8,128)S(1)}, ...), condition=%wide.region_7.7_spmd, body=%wide.region_5.6_spmd.sunk | while | flops 6724631 | bytes 8630401 | solution.py:170
  403.6 5.6 collective-permute-done.2
  423.6 5.6 collective-permute-done.2
  433.5 6.4 collective-permute-done.4
  440.2 40.0 %while.134 = (s32[]{:T(128)}, f32[8,16,256]{2,1,0:T(8,128)S(1)}, f32[2,16,256]{2,1,0:T(8,128)S(1)}, f32[2,16,256]{2,1,0:T(8,128)S(1)}, f32[8,16,256]{2,1,0:T(8,1...) while((s32[]{:T(128)}, f32[8,16,256]{2,1,0:T(8,128)S(1)}, ...), condition=%wide.region_7.7_spmd, body=%wide.region_5.6_spmd.sunk | while | flops 6724631 | bytes 8630401 | solution.py:170
  451.7 5.6 collective-permute-done.2
  471.7 5.6 collective-permute-done.2
  481.5 6.4 collective-permute-done.4
  488.2 40.0 %while.134 = (s32[]{:T(128)}, f32[8,16,256]{2,1,0:T(8,128)S(1)}, f32[2,16,256]{2,1,0:T(8,128)S(1)}, f32[2,16,256]{2,1,0:T(8,128)S(1)}, f32[8,16,256]{2,1,0:T(8,1...) while((s32[]{:T(128)}, f32[8,16,256]{2,1,0:T(8,128)S(1)}, ...), condition=%wide.region_7.7_spmd, body=%wide.region_5.6_spmd.sunk | while | flops 6724631 | bytes 8630401 | solution.py:170
  499.7 5.6 collective-permute-done.2
  519.7 5.6 collective-permute-done.2
  529.6 6.4 collective-permute-done.4
  536.3 40.0 %while.134 = (s32[]{:T(128)}, f32[8,16,256]{2,1,0:T(8,128)S(1)}, f32[2,16,256]{2,1,0:T(8,128)S(1)}, f32[2,16,256]{2,1,0:T(8,128)S(1)}, f32[8,16,256]{2,1,0:T(8,1...) while((s32[]{:T(128)}, f32[8,16,256]{2,1,0:T(8,128)S(1)}, ...), condition=%wide.region_7.7_spmd, body=%wide.region_5.6_spmd.sunk | while | flops 6724631 | bytes 8630401 | solution.py:170
  547.8 5.6 collective-permute-done.2
  567.8 5.6 collective-permute-done.2
  577.7 6.4 collective-permute-done.4
  584.3 40.0 %while.134 = (s32[]{:T(128)}, f32[8,16,256]{2,1,0:T(8,128)S(1)}, f32[2,16,256]{2,1,0:T(8,128)S(1)}, f32[2,16,256]{2,1,0:T(8,128)S(1)}, f32[8,16,256]{2,1,0:T(8,1...) while((s32[]{:T(128)}, f32[8,16,256]{2,1,0:T(8,128)S(1)}, ...), condition=%wide.region_7.7_spmd, body=%wide.region_5.6_spmd.sunk | while | flops 6724631 | bytes 8630401 | solution.py:170
  595.8 5.6 collective-permute-done.2
  615.8 5.6 collective-permute-done.2
  625.7 6.4 collective-permute-done.4
  632.4 40.0 %while.134 = (s32[]{:T(128)}, f32[8,16,256]{2,1,0:T(8,128)S(1)}, f32[2,16,256]{2,1,0:T(8,128)S(1)}, f32[2,16,256]{2,1,0:T(8,128)S(1)}, f32[8,16,256]{2,1,0:T(8,1...) while((s32[]{:T(128)}, f32[8,16,256]{2,1,0:T(8,128)S(1)}, ...), condition=%wide.region_7.7_spmd, body=%wide.region_5.6_spmd.sunk | while | flops 6724631 | bytes 8630401 | solution.py:170
  643.9 5.6 collective-permute-done.2
  663.9 5.6 collective-permute-done.2
  673.8 6.4 collective-permute-done.4
  (726 shorter events, 516.8 us)
Async XLA Ops:
  8.3 7.4 %collective-permute-start.7 = (f32[8,18,1]{2,1,0:T(8,128)S(1)}, f32[8,18,1]{2,1,0:T(8,128)S(1)}, u32[]{:S(2)}, u32[]{:S(2)}) collective-permute-start(f32[8,18,1]{2,1,0:T(8,128)S(1)} %get-tuple-element.2416), channel_id=1, source_target_pairs={{0,1},{2,3},{4,5},{6,7},{8,9},{10,11},{12,13},{14,15},{16,17},{18,... | collective-permute-start | bytes 1736 | tf_op jit(solution)/shard_map/while/body/eval_jaxpr/while/body/eval_jaxpr/ppermute | solution.py:25
  69.4 6.9 collective-permute-start.9
  104.9 6.9 collective-permute-start.9
  140.5 7.7 %collective-permute-start.9 = (f32[8,16,256]{2,1,0:T(8,128)S(1)}, f32[8,16,256]{2,1,0:T(8,128)S(1)}, u32[]{:S(2)}, u32[]{:S(2)}) collective-permute-start(f32[8,16,256]{2,1,0:T(8,128)S(1)} %get-tuple-element.2333), channel_id=1, source_target_pairs={{0,4},{4,8},{8,12},{12,16},{16,20},{20,24},{24,28},{1,5},{5,9},{9,... | collective-permute-start | bytes 393224 | tf_op jit(solution)/shard_map/while/body/eval_jaxpr/ppermute | solution.py:37
  177.0 7.8 %collective-permute-start.9 = (f32[8,16,256]{2,1,0:T(8,128)S(1)}, f32[8,16,256]{2,1,0:T(8,128)S(1)}, u32[]{:S(2)}, u32[]{:S(2)}) collective-permute-start(f32[8,16,256]{2,1,0:T(8,128)S(1)} %get-tuple-element.2333), channel_id=1, source_target_pairs={{0,4},{4,8},{8,12},{12,16},{16,20},{20,24},{24,28},{1,5},{5,9},{9,... | collective-permute-start | bytes 393224 | tf_op jit(solution)/shard_map/while/body/eval_jaxpr/ppermute | solution.py:37
  213.4 7.8 %collective-permute-start.9 = (f32[8,16,256]{2,1,0:T(8,128)S(1)}, f32[8,16,256]{2,1,0:T(8,128)S(1)}, u32[]{:S(2)}, u32[]{:S(2)}) collective-permute-start(f32[8,16,256]{2,1,0:T(8,128)S(1)} %get-tuple-element.2333), channel_id=1, source_target_pairs={{0,4},{4,8},{8,12},{12,16},{16,20},{20,24},{24,28},{1,5},{5,9},{9,... | collective-permute-start | bytes 393224 | tf_op jit(solution)/shard_map/while/body/eval_jaxpr/ppermute | solution.py:37
  249.9 7.8 %collective-permute-start.9 = (f32[8,16,256]{2,1,0:T(8,128)S(1)}, f32[8,16,256]{2,1,0:T(8,128)S(1)}, u32[]{:S(2)}, u32[]{:S(2)}) collective-permute-start(f32[8,16,256]{2,1,0:T(8,128)S(1)} %get-tuple-element.2333), channel_id=1, source_target_pairs={{0,4},{4,8},{8,12},{12,16},{16,20},{20,24},{24,28},{1,5},{5,9},{9,... | collective-permute-start | bytes 393224 | tf_op jit(solution)/shard_map/while/body/eval_jaxpr/ppermute | solution.py:37
  286.4 7.8 %collective-permute-start.9 = (f32[8,16,256]{2,1,0:T(8,128)S(1)}, f32[8,16,256]{2,1,0:T(8,128)S(1)}, u32[]{:S(2)}, u32[]{:S(2)}) collective-permute-start(f32[8,16,256]{2,1,0:T(8,128)S(1)} %get-tuple-element.2333), channel_id=1, source_target_pairs={{0,4},{4,8},{8,12},{12,16},{16,20},{20,24},{24,28},{1,5},{5,9},{9,... | collective-permute-start | bytes 393224 | tf_op jit(solution)/shard_map/while/body/eval_jaxpr/ppermute | solution.py:37
  300.7 11.4 %collective-permute-start.2 = (f32[25,18,1]{2,1,0:T(8,128)S(1)}, f32[25,18,1]{2,1,0:T(8,128)S(1)}, u32[]{:S(2)}, u32[]{:S(2)}) collective-permute-start(f32[25,18,1]{2,1,0:T(8,128)S(1)} %get-tuple-element.2387), channel_id=1, source_target_pairs={{1,0},{3,2},{5,4},{7,6},{9,8},{11,10},{13,12},{15,14},{17,16},{19,... | collective-permute-start | bytes 5408 | tf_op jit(solution)/shard_map/while/body/eval_jaxpr/while/body/eval_jaxpr/ppermute | solution.py:27
  302.0 11.3 %collective-permute-start.3 = (f32[25,18,1]{2,1,0:T(8,128)S(1)}, f32[25,18,1]{2,1,0:T(8,128)S(1)}, u32[]{:S(2)}, u32[]{:S(2)}) collective-permute-start(f32[25,18,1]{2,1,0:T(8,128)S(1)} %get-tuple-element.2388), channel_id=1, source_target_pairs={{0,1},{2,3},{4,5},{6,7},{8,9},{10,11},{12,13},{14,15},{16,17},{18,... | collective-permute-start | bytes 5408 | tf_op jit(solution)/shard_map/while/body/eval_jaxpr/while/body/eval_jaxpr/ppermute | solution.py:25
  320.6 11.5 %collective-permute-start.2 = (f32[25,18,1]{2,1,0:T(8,128)S(1)}, f32[25,18,1]{2,1,0:T(8,128)S(1)}, u32[]{:S(2)}, u32[]{:S(2)}) collective-permute-start(f32[25,18,1]{2,1,0:T(8,128)S(1)} %get-tuple-element.2387), channel_id=1, source_target_pairs={{1,0},{3,2},{5,4},{7,6},{9,8},{11,10},{13,12},{15,14},{17,16},{19,... | collective-permute-start | bytes 5408 | tf_op jit(solution)/shard_map/while/body/eval_jaxpr/while/body/eval_jaxpr/ppermute | solution.py:27
  321.9 11.4 %collective-permute-start.3 = (f32[25,18,1]{2,1,0:T(8,128)S(1)}, f32[25,18,1]{2,1,0:T(8,128)S(1)}, u32[]{:S(2)}, u32[]{:S(2)}) collective-permute-start(f32[25,18,1]{2,1,0:T(8,128)S(1)} %get-tuple-element.2388), channel_id=1, source_target_pairs={{0,1},{2,3},{4,5},{6,7},{8,9},{10,11},{12,13},{14,15},{16,17},{18,... | collective-permute-start | bytes 5408 | tf_op jit(solution)/shard_map/while/body/eval_jaxpr/while/body/eval_jaxpr/ppermute | solution.py:25
  335.0 8.3 %collective-permute-start.4 = (f32[8,16,256]{2,1,0:T(8,128)S(1)}, f32[8,16,256]{2,1,0:T(8,128)S(1)}, u32[]{:S(2)}, u32[]{:S(2)}) collective-permute-start(f32[8,16,256]{2,1,0:T(8,128)S(1)} %get-tuple-element.2362), channel_id=1, source_target_pairs={{4,0},{8,4},{12,8},{16,12},{20,16},{24,20},{28,24},{5,1},{9,5},{13... | collective-permute-start | bytes 393224 | tf_op jit(solution)/shard_map/while/body/eval_jaxpr/ppermute | solution.py:37
  349.2 11.5 %collective-permute-start.2 = (f32[25,18,1]{2,1,0:T(8,128)S(1)}, f32[25,18,1]{2,1,0:T(8,128)S(1)}, u32[]{:S(2)}, u32[]{:S(2)}) collective-permute-start(f32[25,18,1]{2,1,0:T(8,128)S(1)} %get-tuple-element.2387), channel_id=1, source_target_pairs={{1,0},{3,2},{5,4},{7,6},{9,8},{11,10},{13,12},{15,14},{17,16},{19,... | collective-permute-start | bytes 5408 | tf_op jit(solution)/shard_map/while/body/eval_jaxpr/while/body/eval_jaxpr/ppermute | solution.py:27
  350.5 11.4 %collective-permute-start.3 = (f32[25,18,1]{2,1,0:T(8,128)S(1)}, f32[25,18,1]{2,1,0:T(8,128)S(1)}, u32[]{:S(2)}, u32[]{:S(2)}) collective-permute-start(f32[25,18,1]{2,1,0:T(8,128)S(1)} %get-tuple-element.2388), channel_id=1, source_target_pairs={{0,1},{2,3},{4,5},{6,7},{8,9},{10,11},{12,13},{14,15},{16,17},{18,... | collective-permute-start | bytes 5408 | tf_op jit(solution)/shard_map/while/body/eval_jaxpr/while/body/eval_jaxpr/ppermute | solution.py:25
  369.2 11.5 %collective-permute-start.2 = (f32[25,18,1]{2,1,0:T(8,128)S(1)}, f32[25,18,1]{2,1,0:T(8,128)S(1)}, u32[]{:S(2)}, u32[]{:S(2)}) collective-permute-start(f32[25,18,1]{2,1,0:T(8,128)S(1)} %get-tuple-element.2387), channel_id=1, source_target_pairs={{1,0},{3,2},{5,4},{7,6},{9,8},{11,10},{13,12},{15,14},{17,16},{19,... | collective-permute-start | bytes 5408 | tf_op jit(solution)/shard_map/while/body/eval_jaxpr/while/body/eval_jaxpr/ppermute | solution.py:27
  370.5 11.4 %collective-permute-start.3 = (f32[25,18,1]{2,1,0:T(8,128)S(1)}, f32[25,18,1]{2,1,0:T(8,128)S(1)}, u32[]{:S(2)}, u32[]{:S(2)}) collective-permute-start(f32[25,18,1]{2,1,0:T(8,128)S(1)} %get-tuple-element.2388), channel_id=1, source_target_pairs={{0,1},{2,3},{4,5},{6,7},{8,9},{10,11},{12,13},{14,15},{16,17},{18,... | collective-permute-start | bytes 5408 | tf_op jit(solution)/shard_map/while/body/eval_jaxpr/while/body/eval_jaxpr/ppermute | solution.py:25
  383.6 8.3 %collective-permute-start.4 = (f32[8,16,256]{2,1,0:T(8,128)S(1)}, f32[8,16,256]{2,1,0:T(8,128)S(1)}, u32[]{:S(2)}, u32[]{:S(2)}) collective-permute-start(f32[8,16,256]{2,1,0:T(8,128)S(1)} %get-tuple-element.2362), channel_id=1, source_target_pairs={{4,0},{8,4},{12,8},{16,12},{20,16},{24,20},{28,24},{5,1},{9,5},{13... | collective-permute-start | bytes 393224 | tf_op jit(solution)/shard_map/while/body/eval_jaxpr/ppermute | solution.py:37
  397.7 11.5 %collective-permute-start.2 = (f32[25,18,1]{2,1,0:T(8,128)S(1)}, f32[25,18,1]{2,1,0:T(8,128)S(1)}, u32[]{:S(2)}, u32[]{:S(2)}) collective-permute-start(f32[25,18,1]{2,1,0:T(8,128)S(1)} %get-tuple-element.2387), channel_id=1, source_target_pairs={{1,0},{3,2},{5,4},{7,6},{9,8},{11,10},{13,12},{15,14},{17,16},{19,... | collective-permute-start | bytes 5408 | tf_op jit(solution)/shard_map/while/body/eval_jaxpr/while/body/eval_jaxpr/ppermute | solution.py:27
  399.0 11.4 %collective-permute-start.3 = (f32[25,18,1]{2,1,0:T(8,128)S(1)}, f32[25,18,1]{2,1,0:T(8,128)S(1)}, u32[]{:S(2)}, u32[]{:S(2)}) collective-permute-start(f32[25,18,1]{2,1,0:T(8,128)S(1)} %get-tuple-element.2388), channel_id=1, source_target_pairs={{0,1},{2,3},{4,5},{6,7},{8,9},{10,11},{12,13},{14,15},{16,17},{18,... | collective-permute-start | bytes 5408 | tf_op jit(solution)/shard_map/while/body/eval_jaxpr/while/body/eval_jaxpr/ppermute | solution.py:25
  417.7 11.5 %collective-permute-start.2 = (f32[25,18,1]{2,1,0:T(8,128)S(1)}, f32[25,18,1]{2,1,0:T(8,128)S(1)}, u32[]{:S(2)}, u32[]{:S(2)}) collective-permute-start(f32[25,18,1]{2,1,0:T(8,128)S(1)} %get-tuple-element.2387), channel_id=1, source_target_pairs={{1,0},{3,2},{5,4},{7,6},{9,8},{11,10},{13,12},{15,14},{17,16},{19,... | collective-permute-start | bytes 5408 | tf_op jit(solution)/shard_map/while/body/eval_jaxpr/while/body/eval_jaxpr/ppermute | solution.py:27
  419.0 11.4 %collective-permute-start.3 = (f32[25,18,1]{2,1,0:T(8,128)S(1)}, f32[25,18,1]{2,1,0:T(8,128)S(1)}, u32[]{:S(2)}, u32[]{:S(2)}) collective-permute-start(f32[25,18,1]{2,1,0:T(8,128)S(1)} %get-tuple-element.2388), channel_id=1, source_target_pairs={{0,1},{2,3},{4,5},{6,7},{8,9},{10,11},{12,13},{14,15},{16,17},{18,... | collective-permute-start | bytes 5408 | tf_op jit(solution)/shard_map/while/body/eval_jaxpr/while/body/eval_jaxpr/ppermute | solution.py:25
  432.2 7.8 %collective-permute-start.4 = (f32[8,16,256]{2,1,0:T(8,128)S(1)}, f32[8,16,256]{2,1,0:T(8,128)S(1)}, u32[]{:S(2)}, u32[]{:S(2)}) collective-permute-start(f32[8,16,256]{2,1,0:T(8,128)S(1)} %get-tuple-element.2362), channel_id=1, source_target_pairs={{4,0},{8,4},{12,8},{16,12},{20,16},{24,20},{28,24},{5,1},{9,5},{13... | collective-permute-start | bytes 393224 | tf_op jit(solution)/shard_map/while/body/eval_jaxpr/ppermute | solution.py:37
  445.8 11.5 %collective-permute-start.2 = (f32[25,18,1]{2,1,0:T(8,128)S(1)}, f32[25,18,1]{2,1,0:T(8,128)S(1)}, u32[]{:S(2)}, u32[]{:S(2)}) collective-permute-start(f32[25,18,1]{2,1,0:T(8,128)S(1)} %get-tuple-element.2387), channel_id=1, source_target_pairs={{1,0},{3,2},{5,4},{7,6},{9,8},{11,10},{13,12},{15,14},{17,16},{19,... | collective-permute-start | bytes 5408 | tf_op jit(solution)/shard_map/while/body/eval_jaxpr/while/body/eval_jaxpr/ppermute | solution.py:27
  447.1 11.4 %collective-permute-start.3 = (f32[25,18,1]{2,1,0:T(8,128)S(1)}, f32[25,18,1]{2,1,0:T(8,128)S(1)}, u32[]{:S(2)}, u32[]{:S(2)}) collective-permute-start(f32[25,18,1]{2,1,0:T(8,128)S(1)} %get-tuple-element.2388), channel_id=1, source_target_pairs={{0,1},{2,3},{4,5},{6,7},{8,9},{10,11},{12,13},{14,15},{16,17},{18,... | collective-permute-start | bytes 5408 | tf_op jit(solution)/shard_map/while/body/eval_jaxpr/while/body/eval_jaxpr/ppermute | solution.py:25
  465.8 11.5 %collective-permute-start.2 = (f32[25,18,1]{2,1,0:T(8,128)S(1)}, f32[25,18,1]{2,1,0:T(8,128)S(1)}, u32[]{:S(2)}, u32[]{:S(2)}) collective-permute-start(f32[25,18,1]{2,1,0:T(8,128)S(1)} %get-tuple-element.2387), channel_id=1, source_target_pairs={{1,0},{3,2},{5,4},{7,6},{9,8},{11,10},{13,12},{15,14},{17,16},{19,... | collective-permute-start | bytes 5408 | tf_op jit(solution)/shard_map/while/body/eval_jaxpr/while/body/eval_jaxpr/ppermute | solution.py:27
  467.1 11.4 %collective-permute-start.3 = (f32[25,18,1]{2,1,0:T(8,128)S(1)}, f32[25,18,1]{2,1,0:T(8,128)S(1)}, u32[]{:S(2)}, u32[]{:S(2)}) collective-permute-start(f32[25,18,1]{2,1,0:T(8,128)S(1)} %get-tuple-element.2388), channel_id=1, source_target_pairs={{0,1},{2,3},{4,5},{6,7},{8,9},{10,11},{12,13},{14,15},{16,17},{18,... | collective-permute-start | bytes 5408 | tf_op jit(solution)/shard_map/while/body/eval_jaxpr/while/body/eval_jaxpr/ppermute | solution.py:25
  480.2 7.8 %collective-permute-start.4 = (f32[8,16,256]{2,1,0:T(8,128)S(1)}, f32[8,16,256]{2,1,0:T(8,128)S(1)}, u32[]{:S(2)}, u32[]{:S(2)}) collective-permute-start(f32[8,16,256]{2,1,0:T(8,128)S(1)} %get-tuple-element.2362), channel_id=1, source_target_pairs={{4,0},{8,4},{12,8},{16,12},{20,16},{24,20},{28,24},{5,1},{9,5},{13... | collective-permute-start | bytes 393224 | tf_op jit(solution)/shard_map/while/body/eval_jaxpr/ppermute | solution.py:37
  493.8 11.5 %collective-permute-start.2 = (f32[25,18,1]{2,1,0:T(8,128)S(1)}, f32[25,18,1]{2,1,0:T(8,128)S(1)}, u32[]{:S(2)}, u32[]{:S(2)}) collective-permute-start(f32[25,18,1]{2,1,0:T(8,128)S(1)} %get-tuple-element.2387), channel_id=1, source_target_pairs={{1,0},{3,2},{5,4},{7,6},{9,8},{11,10},{13,12},{15,14},{17,16},{19,... | collective-permute-start | bytes 5408 | tf_op jit(solution)/shard_map/while/body/eval_jaxpr/while/body/eval_jaxpr/ppermute | solution.py:27
  495.1 11.4 %collective-permute-start.3 = (f32[25,18,1]{2,1,0:T(8,128)S(1)}, f32[25,18,1]{2,1,0:T(8,128)S(1)}, u32[]{:S(2)}, u32[]{:S(2)}) collective-permute-start(f32[25,18,1]{2,1,0:T(8,128)S(1)} %get-tuple-element.2388), channel_id=1, source_target_pairs={{0,1},{2,3},{4,5},{6,7},{8,9},{10,11},{12,13},{14,15},{16,17},{18,... | collective-permute-start | bytes 5408 | tf_op jit(solution)/shard_map/while/body/eval_jaxpr/while/body/eval_jaxpr/ppermute | solution.py:25
  513.8 11.5 %collective-permute-start.2 = (f32[25,18,1]{2,1,0:T(8,128)S(1)}, f32[25,18,1]{2,1,0:T(8,128)S(1)}, u32[]{:S(2)}, u32[]{:S(2)}) collective-permute-start(f32[25,18,1]{2,1,0:T(8,128)S(1)} %get-tuple-element.2387), channel_id=1, source_target_pairs={{1,0},{3,2},{5,4},{7,6},{9,8},{11,10},{13,12},{15,14},{17,16},{19,... | collective-permute-start | bytes 5408 | tf_op jit(solution)/shard_map/while/body/eval_jaxpr/while/body/eval_jaxpr/ppermute | solution.py:27
  515.1 11.4 %collective-permute-start.3 = (f32[25,18,1]{2,1,0:T(8,128)S(1)}, f32[25,18,1]{2,1,0:T(8,128)S(1)}, u32[]{:S(2)}, u32[]{:S(2)}) collective-permute-start(f32[25,18,1]{2,1,0:T(8,128)S(1)} %get-tuple-element.2388), channel_id=1, source_target_pairs={{0,1},{2,3},{4,5},{6,7},{8,9},{10,11},{12,13},{14,15},{16,17},{18,... | collective-permute-start | bytes 5408 | tf_op jit(solution)/shard_map/while/body/eval_jaxpr/while/body/eval_jaxpr/ppermute | solution.py:25
  528.3 7.8 %collective-permute-start.4 = (f32[8,16,256]{2,1,0:T(8,128)S(1)}, f32[8,16,256]{2,1,0:T(8,128)S(1)}, u32[]{:S(2)}, u32[]{:S(2)}) collective-permute-start(f32[8,16,256]{2,1,0:T(8,128)S(1)} %get-tuple-element.2362), channel_id=1, source_target_pairs={{4,0},{8,4},{12,8},{16,12},{20,16},{24,20},{28,24},{5,1},{9,5},{13... | collective-permute-start | bytes 393224 | tf_op jit(solution)/shard_map/while/body/eval_jaxpr/ppermute | solution.py:37
  541.9 11.5 %collective-permute-start.2 = (f32[25,18,1]{2,1,0:T(8,128)S(1)}, f32[25,18,1]{2,1,0:T(8,128)S(1)}, u32[]{:S(2)}, u32[]{:S(2)}) collective-permute-start(f32[25,18,1]{2,1,0:T(8,128)S(1)} %get-tuple-element.2387), channel_id=1, source_target_pairs={{1,0},{3,2},{5,4},{7,6},{9,8},{11,10},{13,12},{15,14},{17,16},{19,... | collective-permute-start | bytes 5408 | tf_op jit(solution)/shard_map/while/body/eval_jaxpr/while/body/eval_jaxpr/ppermute | solution.py:27
  543.2 11.4 %collective-permute-start.3 = (f32[25,18,1]{2,1,0:T(8,128)S(1)}, f32[25,18,1]{2,1,0:T(8,128)S(1)}, u32[]{:S(2)}, u32[]{:S(2)}) collective-permute-start(f32[25,18,1]{2,1,0:T(8,128)S(1)} %get-tuple-element.2388), channel_id=1, source_target_pairs={{0,1},{2,3},{4,5},{6,7},{8,9},{10,11},{12,13},{14,15},{16,17},{18,... | collective-permute-start | bytes 5408 | tf_op jit(solution)/shard_map/while/body/eval_jaxpr/while/body/eval_jaxpr/ppermute | solution.py:25
  561.9 11.5 %collective-permute-start.2 = (f32[25,18,1]{2,1,0:T(8,128)S(1)}, f32[25,18,1]{2,1,0:T(8,128)S(1)}, u32[]{:S(2)}, u32[]{:S(2)}) collective-permute-start(f32[25,18,1]{2,1,0:T(8,128)S(1)} %get-tuple-element.2387), channel_id=1, source_target_pairs={{1,0},{3,2},{5,4},{7,6},{9,8},{11,10},{13,12},{15,14},{17,16},{19,... | collective-permute-start | bytes 5408 | tf_op jit(solution)/shard_map/while/body/eval_jaxpr/while/body/eval_jaxpr/ppermute | solution.py:27
  563.2 11.4 %collective-permute-start.3 = (f32[25,18,1]{2,1,0:T(8,128)S(1)}, f32[25,18,1]{2,1,0:T(8,128)S(1)}, u32[]{:S(2)}, u32[]{:S(2)}) collective-permute-start(f32[25,18,1]{2,1,0:T(8,128)S(1)} %get-tuple-element.2388), channel_id=1, source_target_pairs={{0,1},{2,3},{4,5},{6,7},{8,9},{10,11},{12,13},{14,15},{16,17},{18,... | collective-permute-start | bytes 5408 | tf_op jit(solution)/shard_map/while/body/eval_jaxpr/while/body/eval_jaxpr/ppermute | solution.py:25
  576.3 7.8 %collective-permute-start.4 = (f32[8,16,256]{2,1,0:T(8,128)S(1)}, f32[8,16,256]{2,1,0:T(8,128)S(1)}, u32[]{:S(2)}, u32[]{:S(2)}) collective-permute-start(f32[8,16,256]{2,1,0:T(8,128)S(1)} %get-tuple-element.2362), channel_id=1, source_target_pairs={{4,0},{8,4},{12,8},{16,12},{20,16},{24,20},{28,24},{5,1},{9,5},{13... | collective-permute-start | bytes 393224 | tf_op jit(solution)/shard_map/while/body/eval_jaxpr/ppermute | solution.py:37
  589.9 11.5 %collective-permute-start.2 = (f32[25,18,1]{2,1,0:T(8,128)S(1)}, f32[25,18,1]{2,1,0:T(8,128)S(1)}, u32[]{:S(2)}, u32[]{:S(2)}) collective-permute-start(f32[25,18,1]{2,1,0:T(8,128)S(1)} %get-tuple-element.2387), channel_id=1, source_target_pairs={{1,0},{3,2},{5,4},{7,6},{9,8},{11,10},{13,12},{15,14},{17,16},{19,... | collective-permute-start | bytes 5408 | tf_op jit(solution)/shard_map/while/body/eval_jaxpr/while/body/eval_jaxpr/ppermute | solution.py:27
  591.2 11.4 %collective-permute-start.3 = (f32[25,18,1]{2,1,0:T(8,128)S(1)}, f32[25,18,1]{2,1,0:T(8,128)S(1)}, u32[]{:S(2)}, u32[]{:S(2)}) collective-permute-start(f32[25,18,1]{2,1,0:T(8,128)S(1)} %get-tuple-element.2388), channel_id=1, source_target_pairs={{0,1},{2,3},{4,5},{6,7},{8,9},{10,11},{12,13},{14,15},{16,17},{18,... | collective-permute-start | bytes 5408 | tf_op jit(solution)/shard_map/while/body/eval_jaxpr/while/body/eval_jaxpr/ppermute | solution.py:25
  609.9 11.5 %collective-permute-start.2 = (f32[25,18,1]{2,1,0:T(8,128)S(1)}, f32[25,18,1]{2,1,0:T(8,128)S(1)}, u32[]{:S(2)}, u32[]{:S(2)}) collective-permute-start(f32[25,18,1]{2,1,0:T(8,128)S(1)} %get-tuple-element.2387), channel_id=1, source_target_pairs={{1,0},{3,2},{5,4},{7,6},{9,8},{11,10},{13,12},{15,14},{17,16},{19,... | collective-permute-start | bytes 5408 | tf_op jit(solution)/shard_map/while/body/eval_jaxpr/while/body/eval_jaxpr/ppermute | solution.py:27
  611.2 11.4 %collective-permute-start.3 = (f32[25,18,1]{2,1,0:T(8,128)S(1)}, f32[25,18,1]{2,1,0:T(8,128)S(1)}, u32[]{:S(2)}, u32[]{:S(2)}) collective-permute-start(f32[25,18,1]{2,1,0:T(8,128)S(1)} %get-tuple-element.2388), channel_id=1, source_target_pairs={{0,1},{2,3},{4,5},{6,7},{8,9},{10,11},{12,13},{14,15},{16,17},{18,... | collective-permute-start | bytes 5408 | tf_op jit(solution)/shard_map/while/body/eval_jaxpr/while/body/eval_jaxpr/ppermute | solution.py:25
  624.4 7.8 %collective-permute-start.4 = (f32[8,16,256]{2,1,0:T(8,128)S(1)}, f32[8,16,256]{2,1,0:T(8,128)S(1)}, u32[]{:S(2)}, u32[]{:S(2)}) collective-permute-start(f32[8,16,256]{2,1,0:T(8,128)S(1)} %get-tuple-element.2362), channel_id=1, source_target_pairs={{4,0},{8,4},{12,8},{16,12},{20,16},{24,20},{28,24},{5,1},{9,5},{13... | collective-permute-start | bytes 393224 | tf_op jit(solution)/shard_map/while/body/eval_jaxpr/ppermute | solution.py:37
  638.0 11.5 %collective-permute-start.2 = (f32[25,18,1]{2,1,0:T(8,128)S(1)}, f32[25,18,1]{2,1,0:T(8,128)S(1)}, u32[]{:S(2)}, u32[]{:S(2)}) collective-permute-start(f32[25,18,1]{2,1,0:T(8,128)S(1)} %get-tuple-element.2387), channel_id=1, source_target_pairs={{1,0},{3,2},{5,4},{7,6},{9,8},{11,10},{13,12},{15,14},{17,16},{19,... | collective-permute-start | bytes 5408 | tf_op jit(solution)/shard_map/while/body/eval_jaxpr/while/body/eval_jaxpr/ppermute | solution.py:27
  639.3 11.4 %collective-permute-start.3 = (f32[25,18,1]{2,1,0:T(8,128)S(1)}, f32[25,18,1]{2,1,0:T(8,128)S(1)}, u32[]{:S(2)}, u32[]{:S(2)}) collective-permute-start(f32[25,18,1]{2,1,0:T(8,128)S(1)} %get-tuple-element.2388), channel_id=1, source_target_pairs={{0,1},{2,3},{4,5},{6,7},{8,9},{10,11},{12,13},{14,15},{16,17},{18,... | collective-permute-start | bytes 5408 | tf_op jit(solution)/shard_map/while/body/eval_jaxpr/while/body/eval_jaxpr/ppermute | solution.py:25
  658.0 11.5 %collective-permute-start.2 = (f32[25,18,1]{2,1,0:T(8,128)S(1)}, f32[25,18,1]{2,1,0:T(8,128)S(1)}, u32[]{:S(2)}, u32[]{:S(2)}) collective-permute-start(f32[25,18,1]{2,1,0:T(8,128)S(1)} %get-tuple-element.2387), channel_id=1, source_target_pairs={{1,0},{3,2},{5,4},{7,6},{9,8},{11,10},{13,12},{15,14},{17,16},{19,... | collective-permute-start | bytes 5408 | tf_op jit(solution)/shard_map/while/body/eval_jaxpr/while/body/eval_jaxpr/ppermute | solution.py:27
  659.3 11.4 %collective-permute-start.3 = (f32[25,18,1]{2,1,0:T(8,128)S(1)}, f32[25,18,1]{2,1,0:T(8,128)S(1)}, u32[]{:S(2)}, u32[]{:S(2)}) collective-permute-start(f32[25,18,1]{2,1,0:T(8,128)S(1)} %get-tuple-element.2388), channel_id=1, source_target_pairs={{0,1},{2,3},{4,5},{6,7},{8,9},{10,11},{12,13},{14,15},{16,17},{18,... | collective-permute-start | bytes 5408 | tf_op jit(solution)/shard_map/while/body/eval_jaxpr/while/body/eval_jaxpr/ppermute | solution.py:25
  672.4 7.8 %collective-permute-start.4 = (f32[8,16,256]{2,1,0:T(8,128)S(1)}, f32[8,16,256]{2,1,0:T(8,128)S(1)}, u32[]{:S(2)}, u32[]{:S(2)}) collective-permute-start(f32[8,16,256]{2,1,0:T(8,128)S(1)} %get-tuple-element.2362), channel_id=1, source_target_pairs={{4,0},{8,4},{12,8},{16,12},{20,16},{24,20},{28,24},{5,1},{9,5},{13... | collective-permute-start | bytes 393224 | tf_op jit(solution)/shard_map/while/body/eval_jaxpr/ppermute | solution.py:37
  (103 other events, 459.1 us)
where the time goes:
time: 699 us; the launch traced here: 696 us
  starting transfers between devices  336 us (48%)
  waiting for transfers between devices  299 us (43%)
  other arithmetic  49 us (7%)
    ppermute x66, starting transfers between devices, padded(): lax.ppermute(tail, axis, [(i, (i + 1) % count) for i in range(ends)])  202 us
    ppermute x66, waiting for transfers between devices, padded(): lax.ppermute(head, axis, [((i + 1) % count, i) for i in range(ends)])  162 us
    ppermute x66, starting transfers between devices, padded(): lax.ppermute(head, axis, [((i + 1) % count, i) for i in range(ends)])  85.2 us
    ppermute x16, waiting for transfers between devices, passed_along(): lax.ppermute(value, axis, [(source, source + steps) for source in range(i...  70.2 us
    ppermute x66, waiting for transfers between devices, padded(): lax.ppermute(tail, axis, [(i, (i + 1) % count) for i in range(ends)])  66.6 us
    ppermute x16, starting transfers between devices, passed_along(): lax.ppermute(value, axis, [(source, source + steps) for source in range(i...  48.7 us
    concatenate x66, other arithmetic, padded(): jnp.concatenate([lax.ppermute(tail, axis, [(i, (i + 1) % count) for i in...  14.2 us
  transfers between devices with their start and end apart: 148, of which 115 were waited for; matrix products, arithmetic and copies ran while one was open for 0% of the time, Pallas kernels for 0%

commit v1 on v0

--- a/solution.py
+++ b/solution.py
@@ -1,8 +1,11 @@
+import functools
 import math
 
 import jax
 import jax.numpy as jnp
 from jax import lax
+from jax.experimental import pallas as pl
+from jax.experimental.pallas import tpu as pltpu
 from jax.sharding import PartitionSpec as P
 
 SOFTMIN_TEMPER = 0.5
@@ -47,7 +50,7 @@
     return lowest - SOFTMIN_TEMPER * jnp.log(total)
 
 
-def local(slowness, air_mask, reflector, shot_cells, receiver_mask, residual):
+def local_generic(slowness, air_mask, reflector, shot_cells, receiver_mask, residual):
     depth_count = lax.axis_size("depth")
     depth_pos = lax.axis_index("depth")
     cz, shift_along_x, shift_along_y = slowness.shape
@@ -200,6 +203,172 @@
     return 0.5 * raw + 0.0625 * beside_all
 
 
+WIDE = 128
+OWN = 64
+ROOT2 = math.sqrt(2.0)
+ROOT3 = math.sqrt(3.0)
+
+
+def left(cells):
+    return pltpu.roll(cells, 1, axis=1)
+
+
+def right(cells):
+    return pltpu.roll(cells, cells.shape[1] - 1, axis=1)
+
+
+def above(cells):
+    return pltpu.roll(cells, 1, axis=0)
+
+
+def below(cells):
+    return pltpu.roll(cells, cells.shape[0] - 1, axis=0)
+
+
+def window_columns(shape, tile, half):
+    lane = lax.broadcasted_iota(jnp.int32, shape, 1)
+    shift = jnp.where(
+        half == 0,
+        jnp.where(lane >= 96, -WIDE, 0),
+        jnp.where(lane < 32, WIDE, 0),
+    )
+    return tile * WIDE + lane + shift
+
+
+def stencil_factors(factors, shot_cells_ref, pair, tile, half, nx, ny):
+    shape = (2 * nx, WIDE)
+    row = lax.broadcasted_iota(jnp.int32, shape, 0)
+    second = row >= nx
+    row = jnp.where(second, row - nx, row)
+    col = window_columns(shape, tile, half)
+    place = [
+        jnp.where(second, shot_cells_ref[2 * pair + 1, d], shot_cells_ref[2 * pair, d]).astype(
+            jnp.float32
+        )
+        for d in (0, 1)
+    ]
+
+    def surface(a, b):
+        u = (row + a).astype(jnp.float32) - place[0]
+        v = (col + b).astype(jnp.float32) - place[1]
+        return SURF * jnp.sqrt(u * u + v * v)
+
+    here = surface(0, 0)
+    for slot, (a, b) in enumerate(((0, -1), (0, 1), (-1, 0), (1, 0))):
+        inside = (row + a >= 0) & (row + a < nx) & (col + b >= 0) & (col + b < ny)
+        beside = surface(a, b)
+        penalty = jnp.where(inside, jnp.float32(0.0), jnp.float32(STEP_PENALTY))
+        value = jnp.where(inside, beside, jnp.float32(0.0))
+        factors[slot] = jnp.exp(-((value + penalty) - here) / SOFTMIN_TEMPER)
+        factors[4 + slot] = jnp.where(inside, jnp.exp(-(here - beside) / SOFTMIN_TEMPER), 0.0)
+
+
+def twice(cells):
+    return jnp.concatenate([cells, cells], axis=0)
+
+
+def forward_plane(k, speed, front, factors, fronts, spans):
+    w1 = twice(jnp.exp(-speed / SOFTMIN_TEMPER))
+    w2 = twice(jnp.exp(-(speed * ROOT2) / SOFTMIN_TEMPER))
+    w3 = twice(jnp.exp(-(speed * ROOT3) / SOFTMIN_TEMPER))
+    side = factors[0] * left(front) + factors[1] * right(front)
+    edge = side + factors[2] * above(front) + factors[3] * below(front)
+    corner = factors[2] * above(side) + factors[3] * below(side)
+    one, two, three = w1 * front, w2 * edge, w3 * corner
+    front = one + two + three
+    fronts[k] = front
+    spans[k] = one + ROOT2 * two + ROOT3 * three
+    return front
+
+
+def adjoint_plane(k, speed, back, source, reflector, factors, fronts, spans, inside, edges):
+    w1 = twice(jnp.exp(-speed / SOFTMIN_TEMPER))
+    w2 = twice(jnp.exp(-(speed * ROOT2) / SOFTMIN_TEMPER))
+    w3 = twice(jnp.exp(-(speed * ROOT3) / SOFTMIN_TEMPER))
+    lam = jnp.where(twice(reflector == k), source / fronts[k], 0.0) + back
+    part = lam * spans[k] + jnp.where(twice(reflector >= k), source, 0.0)
+    nx = speed.shape[0]
+    raw = jnp.where(inside & (speed != AIR_SLOW), part[:nx] + part[nx:], 0.0)
+    line = raw + left(raw) + right(raw)
+    box = line + jnp.where(edges[0], 0.0, above(line)) + jnp.where(edges[1], 0.0, below(line))
+    grad = 0.4375 * raw + 0.0625 * box
+    two, three = w2 * lam, w3 * lam
+    far = two + factors[4] * left(three) + factors[5] * right(three)
+    back = (
+        w1 * lam
+        + (factors[4] * left(two) + factors[5] * right(two))
+        + (factors[6] * above(far) + factors[7] * below(far))
+    )
+    return back, grad
+
+
+def sweep_kernel(ny, shot_cells_ref, speed_ref, source_ref, reflector_ref, out_ref, factors, fronts, spans):
+    depth = lax.axis_index("depth")
+    half = lax.axis_index("gx")
+    tile = 2 * lax.axis_index("gy") + lax.rem(depth, 2)
+    nz, nx, _ = speed_ref.shape
+    stencil_factors(factors, shot_cells_ref, depth // 2, tile, half, nx, ny)
+
+    def forward(k, front):
+        return forward_plane(k, speed_ref[k], front, factors, fronts, spans)
+
+    lax.fori_loop(0, nz, forward, jnp.ones((2 * nx, WIDE), jnp.float32))
+    source = source_ref[...]
+    reflector = reflector_ref[...]
+    col = window_columns((nx, WIDE), tile, half)
+    row = lax.broadcasted_iota(jnp.int32, (nx, WIDE), 0)
+    lane = lax.broadcasted_iota(jnp.int32, (nx, WIDE), 1)
+    inside = (col >= 0) & (col < ny)
+    mine = (lane // OWN) == half
+
+    def adjoint(step, back):
+        k = nz - 1 - step
+        back, grad = adjoint_plane(
+            k, speed_ref[k], back, source, reflector, factors, fronts, spans, inside, (row == 0, row == nx - 1)
+        )
+        out_ref[k] = jnp.where(mine, grad, 0.0)
+        return back
+
+    lax.fori_loop(0, nz, adjoint, jnp.zeros((2 * nx, WIDE), jnp.float32))
+
+
+def local_split(slowness, air_mask, reflector, shot_cells, receiver_mask, residual):
+    cz, bx, by = slowness.shape
+    nz, nx, ny = cz * lax.axis_size("depth"), bx * lax.axis_size("gx"), by * lax.axis_size("gy")
+    depth = lax.axis_index("depth")
+    tile = 2 * lax.axis_index("gy") + lax.rem(depth, 2)
+    half = lax.axis_index("gx")
+    speed = jnp.where(air_mask == 1, jnp.float32(AIR_SLOW), slowness)
+    speed = lax.all_gather(speed, ("depth",), axis=0, tiled=True)
+    source = jnp.where(receiver_mask == 1, residual, jnp.float32(0.0))
+    source = lax.dynamic_slice_in_dim(source, 2 * (depth // 2), 2, axis=0)
+    fields = jnp.concatenate([speed, source, reflector.astype(jnp.float32)[None]], 0)
+    fields = lax.all_gather(lax.all_gather(fields, "gx", axis=1, tiled=True), "gy", axis=2, tiled=True)
+    near = lax.dynamic_slice_in_dim(fields, tile * WIDE, WIDE, axis=2)
+    other = jnp.clip(tile + 2 * half - 1, 0, ny // WIDE - 1)
+    far = lax.dynamic_slice_in_dim(fields, other * WIDE, WIDE, axis=2)
+    lane = jnp.arange(WIDE)
+    own = jnp.where(half == 0, lane < 96, lane >= 32)
+    fields = jnp.where(own, near, far)
+    out = pl.pallas_call(
+        functools.partial(sweep_kernel, ny),
+        out_shape=jax.ShapeDtypeStruct((nz, nx, WIDE), jnp.float32),
+        in_specs=[pl.BlockSpec(memory_space=pltpu.SMEM)] + [pl.BlockSpec(memory_space=pltpu.VMEM)] * 3,
+        out_specs=pl.BlockSpec(memory_space=pltpu.VMEM),
+        scratch_shapes=[
+            pltpu.VMEM((8, 2 * nx, WIDE), jnp.float32),
+            pltpu.VMEM((nz, 2 * nx, WIDE), jnp.float32),
+            pltpu.VMEM((nz, 2 * nx, WIDE), jnp.float32),
+        ],
+        compiler_params=pltpu.CompilerParams(vmem_limit_bytes=16 * 1024 * 1024),
+    )(shot_cells, fields[:nz], fields[nz : nz + 2].reshape(2 * nx, WIDE), fields[nz + 2].astype(jnp.int32))
+    zero = jnp.zeros_like(out)
+    first = lax.rem(depth, 2) == 0
+    out = jnp.concatenate([jnp.where(first, out, zero), jnp.where(first, zero, out)], axis=2)
+    out = lax.psum_scatter(out, "depth", scatter_dimension=0, tiled=True)
+    return lax.psum_scatter(out, "gx", scatter_dimension=1, tiled=True)
+
+
 def solution(mesh):
     in_specs = (
         P("depth", "gx", "gy"),
@@ -210,4 +379,18 @@
         P(None, "gx", "gy"),
     )
     out_specs = P("depth", "gx", "gy")
-    return jax.shard_map(local, mesh=mesh, in_specs=in_specs, out_specs=out_specs, check_vma=False)
+    sizes = dict(mesh.shape)
+
+    def whole(slowness, air_mask, reflector, shot_cells, receiver_mask, residual):
+        nz, nx, ny = slowness.shape
+        fits = (
+            sizes == {"depth": 8, "gx": 2, "gy": 2}
+            and (nz, nx, ny) == (16, 32, 512)
+            and shot_cells.shape[0] == 8
+        )
+        local = local_split if fits else local_generic
+        return jax.shard_map(local, mesh=mesh, in_specs=in_specs, out_specs=out_specs, check_vma=False)(
+            slowness, air_mask, reflector, shot_cells, receiver_mask, residual
+        )
+
+    return whole

time: 699 us -> 153 us (0.22)
  starting transfers between devices: 336 us -> 0.09 us
  waiting for transfers between devices: 299 us -> 95.3 us
  other arithmetic: 49 us -> 4.34 us
  blocking collectives: 0 us -> 34.9 us
  between operations: 0.16 us -> 13.2 us
    ppermute x148 -> x0, starting transfers between devices: 336 us -> none  [the longest x66 202 us: padded(): lax.ppermute(tail, axis, [(i, (i + 1) % count) for i in range(ends)])]
    ppermute x148 -> x0, waiting for transfers between devices: 299 us -> none  [the longest x66 162 us: padded(): lax.ppermute(head, axis, [((i + 1) % count, i) for i in range(ends)])]
    reduce_scatter x0 -> x2, waiting for transfers between devices: none -> 70.8 us  [the longest x1 62 us: local_split(): out = lax.psum_scatter(out, 'depth', scatter_dimension=0, tiled=True)]
    all_gather x0 -> x2, blocking collectives: none -> 34.9 us  [the longest x1 32.5 us: local_split(): speed = lax.all_gather(speed, ('depth',), axis=0, tiled=True)]
    all_gather x0 -> x1, waiting for transfers between devices: none -> 24.5 us  [local_split(): lax.all_gather(lax.all_gather(fields, 'gx', axis=1, tiled=True), 'gy', ax...]
    concatenate x66 -> x2, other arithmetic: 14.2 us -> 0.85 us  [the longest x1 0.83 us: local_split(): jnp.concatenate([jnp.where(first, out, zero), jnp.where(first, zero, out)...]
    add x91 -> x0, other arithmetic: 9.57 us -> none  [the longest x16 7.92 us: adjoint_plane(): back_new = back_new + lam_from * prob_from]
    reduce_sum x17 -> x0, other arithmetic: 7.81 us -> none  [the longest x16 6.89 us: adjoint_plane(): return (back_new, jnp.sum(lam * weight_sum, axis=0))]
  transfers between devices with their start and end apart: 148 -> 3, of which waited for: 115 -> 3; matrix products, arithmetic and copies ran while one was open for 0% -> 0% of each run, Pallas kernels for 0% -> 0%
where the time goes in v1:
time: 153 us; the launch traced here: 152 us
  waiting for transfers between devices  95.3 us (62%)
  blocking collectives  34.9 us (23%)
  between operations  13.2 us (9%)
  Pallas kernels  4.4 us (3%)
  other arithmetic  4.34 us (3%)
    reduce_scatter x1, waiting for transfers between devices, local_split(): out = lax.psum_scatter(out, 'depth', scatter_dimension=0, tiled=True)  62 us
    all_gather x1, blocking collectives, local_split(): speed = lax.all_gather(speed, ('depth',), axis=0, tiled=True)  32.5 us
    all_gather x1, waiting for transfers between devices, local_split(): lax.all_gather(lax.all_gather(fields, 'gx', axis=1, tiled=True), 'gy', ax...  24.5 us
    reduce_scatter x1, waiting for transfers between devices, local_split(): return lax.psum_scatter(out, 'gx', scatter_dimension=1, tiled=True)  8.74 us
    pallas_call x1, Pallas kernels, local_split(): pl.pallas_call(functools.partial(sweep_kernel, ny), out_shape=jax.ShapeDt...  4.4 us
  transfers between devices with their start and end apart: 3, of which 3 were waited for; matrix products, arithmetic and copies ran while one was open for 0% of the time, Pallas kernels for 0%

profile of v1, /device:TPU:0, one launch (start us, length us, event | category | flops | bytes accessed | tf_op | source)
XLA Modules:
  0.0 152.3 jit_solution(11446624167663932118)
XLA Ops:
  6.5 0.0 all-gather.2.cloned.1.call-start
  6.5 0.8 compare_select_fusion
  7.3 32.5 %all_gather.9 = f32[16,16,256]{2,1,0:T(8,128)S(1)} all-gather(f32[2,16,256]{2,1,0:T(8,128)S(1)} %compare_select_fusion), channel_id=1, replica_groups=mesh['depth'=8,'gx'=2,'gy'=2] {'depth'}, dimensions={0}, use_global_device_ids=true | all-gather | bytes 294912 | tf_op jit(solution)/shard_map/all_gather | solution.py:342
  39.8 0.0 copy-start
  39.8 0.7 convert_bitcast_fusion
  40.6 0.8 dynamic-slice_select_fusion.1
  41.4 2.4 %all_gather.10 = f32[19,32,256]{2,1,0:T(8,128)} all-gather(f32[19,16,256]{2,1,0:T(8,128)S(1)} %pad_maximum_fusion.1), channel_id=1, replica_groups=mesh['depth'=8,'gx'=2,'gy'=2] {'gx'}, dimensions={1}, use_global_device_ids=true | all-gather | bytes 933888 | tf_op jit(solution)/shard_map/all_gather | solution.py:346
  43.8 0.0 all-gather.2.cloned.1.call-update
  43.8 0.0 reduce-scatter.3.cloned.1.call-start
  43.9 0.0 copy-done
  43.9 0.1 copy.8.shot_cells_ref
  44.0 24.5 %all-gather.2.cloned.1.call-done = f32[19,32,512]{2,1,0:T(8,128)} async-done(((f32[19,32,256]{2,1,0:T(8,128)}), f32[19,32,512]{2,1,0:T(8,128)}) %all-gather.2.cloned.1.call-update) | async-done | bytes 1245200 | tf_op jit(solution)/shard_map/all_gather | solution.py:346
  68.4 1.1 dynamic-slice_select_fusion
  69.6 4.4 %shard_map.64 = f32[16,32,128]{2,1,0:T(8,128)S(1)} custom-call(s32[8,2]{1,0:T(8,128)S(1)} %copy.8.shot_cells_ref, f32[16,32,128]{2,1,0:T(8,128)S(1)} %slice.12.speed_ref, f32[64,128]{1,0:T(8,128)S(1)} %bitcast.5, s32[32,128]{1,0:T(8,128)S(1)} %fusion.reflector_ref), custom_call_target="tpu_custom_call" | custom-call | tf_op jit(solution)/shard_map/pallas_call | solution.py:353
  74.0 0.1 broadcast_select_fusion.1
  74.1 0.8 pad_maximum_fusion
  74.9 0.0 reduce-scatter.3.cloned.1.call-update
  75.0 0.0 reduce-scatter.5.cloned.1.call-start
  75.0 62.0 %reduce-scatter.3.cloned.1.call-done = f32[2,32,256]{2,1,0:T(8,128)} async-done(((f32[16,32,256]{2,1,0:T(8,128)}), f32[2,32,256]{2,1,0:T(8,128)}) %reduce-scatter.3.cloned.1.call-update) | async-done | bytes 65552 | tf_op jit(solution)/shard_map/reduce_scatter | solution.py:368
  137.0 0.0 reduce-scatter.5.cloned.1.call-update
  137.1 8.7 %reduce-scatter.5.cloned.1.call-done = f32[2,16,256]{2,1,0:T(8,128)} async-done(((f32[2,32,256]{2,1,0:T(8,128)}), f32[2,16,256]{2,1,0:T(8,128)}) %reduce-scatter.5.cloned.1.call-update) | async-done | bytes 32784 | tf_op jit(solution)/shard_map/reduce_scatter | solution.py:369
  (5 shorter events, 0.1 us)
Async XLA Ops:
  6.5 61.9 %all-gather.2.cloned.1.call-start = ((), (), s32[]{:S(2)}) async-start(), calls=%async_computation.2 | async-start | bytes 1867776 | tf_op jit(solution)/shard_map/all_gather | solution.py:346
  39.8 4.0 %copy-start = (s32[8,2]{0,1:T(2,128)S(1)}, s32[8,2]{0,1:T(2,128)}, u32[]{:S(2)}) copy-start(s32[8,2]{0,1:T(2,128)} %param.9) | copy-start | bytes 196
  43.8 93.2 %reduce-scatter.3.cloned.1.call-start = ((), (), s32[]{:S(2)}) async-start(), calls=%async_computation.3 | async-start | bytes 589824 | tf_op jit(solution)/shard_map/reduce_scatter | solution.py:368
  75.0 70.8 %reduce-scatter.5.cloned.1.call-start = ((), (), s32[]{:S(2)}) async-start(), calls=%async_computation.4 | async-start | bytes 98304 | tf_op jit(solution)/shard_map/reduce_scatter | solution.py:369
Sparse Core Ops, SparseCore 0:
  43.9 24.4 all-gather.1
  75.1 61.9 reduce-scatter.2
  139.3 6.4 reduce-scatter.4

commit v2 on v1

--- a/solution.py
+++ b/solution.py
@@ -205,6 +205,7 @@
 
 WIDE = 128
 OWN = 64
+SIDE = 32
 ROOT2 = math.sqrt(2.0)
 ROOT3 = math.sqrt(3.0)
 
@@ -225,22 +226,25 @@
     return pltpu.roll(cells, cells.shape[0] - 1, axis=0)
 
 
-def window_columns(shape, tile, half):
-    lane = lax.broadcasted_iota(jnp.int32, shape, 1)
-    shift = jnp.where(
-        half == 0,
-        jnp.where(lane >= 96, -WIDE, 0),
-        jnp.where(lane < 32, WIDE, 0),
-    )
-    return tile * WIDE + lane + shift
-
-
-def stencil_factors(factors, shot_cells_ref, pair, tile, half, nx, ny):
+def halfway(cells):
+    return pltpu.roll(cells, OWN, axis=cells.ndim - 1)
+
+
+def lanes(shape):
+    return lax.broadcasted_iota(jnp.int32, shape, len(shape) - 1)
+
+
+def window_columns(shape, part):
+    lane = lanes(shape)
+    return part * OWN + lane - jnp.where(lane >= WIDE - SIDE, WIDE, 0)
+
+
+def stencil_factors(factors, shot_cells_ref, pair, part, nx, ny):
     shape = (2 * nx, WIDE)
     row = lax.broadcasted_iota(jnp.int32, shape, 0)
     second = row >= nx
     row = jnp.where(second, row - nx, row)
-    col = window_columns(shape, tile, half)
+    col = window_columns(shape, part)
     place = [
         jnp.where(second, shot_cells_ref[2 * pair + 1, d], shot_cells_ref[2 * pair, d]).astype(
             jnp.float32
@@ -285,8 +289,9 @@
     w1 = twice(jnp.exp(-speed / SOFTMIN_TEMPER))
     w2 = twice(jnp.exp(-(speed * ROOT2) / SOFTMIN_TEMPER))
     w3 = twice(jnp.exp(-(speed * ROOT3) / SOFTMIN_TEMPER))
-    lam = jnp.where(twice(reflector == k), source / fronts[k], 0.0) + back
-    part = lam * spans[k] + jnp.where(twice(reflector >= k), source, 0.0)
+    plane = k.astype(jnp.float32)
+    lam = jnp.where(twice(reflector == plane), source / fronts[k], 0.0) + back
+    part = lam * spans[k] + jnp.where(twice(reflector >= plane), source, 0.0)
     nx = speed.shape[0]
     raw = jnp.where(inside & (speed != AIR_SLOW), part[:nx] + part[nx:], 0.0)
     line = raw + left(raw) + right(raw)
@@ -302,71 +307,337 @@
     return back, grad
 
 
-def sweep_kernel(ny, shot_cells_ref, speed_ref, source_ref, reflector_ref, out_ref, factors, fronts, spans):
-    depth = lax.axis_index("depth")
-    half = lax.axis_index("gx")
-    tile = 2 * lax.axis_index("gy") + lax.rem(depth, 2)
-    nz, nx, _ = speed_ref.shape
-    stencil_factors(factors, shot_cells_ref, depth // 2, tile, half, nx, ny)
-
-    def forward(k, front):
-        return forward_plane(k, speed_ref[k], front, factors, fronts, spans)
-
-    lax.fori_loop(0, nz, forward, jnp.ones((2 * nx, WIDE), jnp.float32))
-    source = source_ref[...]
-    reflector = reflector_ref[...]
-    col = window_columns((nx, WIDE), tile, half)
-    row = lax.broadcasted_iota(jnp.int32, (nx, WIDE), 0)
-    lane = lax.broadcasted_iota(jnp.int32, (nx, WIDE), 1)
+def part_window(part, x, first, second, beyond):
+    lane = lanes(first.shape)
+    if part == 0:
+        return jnp.where(lane < WIDE - SIDE, first, jnp.where(x == 1, beyond, first))
+    if part == 1:
+        return halfway(jnp.where(lane >= SIDE, first, second))
+    if part == 2:
+        return jnp.where(lane < WIDE - SIDE, second, first)
+    return halfway(jnp.where(lane >= SIDE, second, jnp.where(x == 0, beyond, second)))
+
+
+def sweep_kernel(
+    ny,
+    shot_cells_ref,
+    slowness_hbm,
+    air_hbm,
+    reflector_hbm,
+    receiver_hbm,
+    residual_hbm,
+    out_ref,
+    slowness,
+    air,
+    reflect,
+    receiver,
+    resid,
+    rim_out,
+    rim_in,
+    wins,
+    speeds,
+    shots_rim_out,
+    shots_rim_in,
+    shots_side,
+    fields,
+    factors,
+    fronts,
+    spans,
+    packed,
+    sibling_sum,
+    both,
+    gathered,
+    load_sem,
+    rim_send,
+    rim_recv,
+    slab_send,
+    slab_recv,
+    pass_send,
+    pass_recv,
+    shots_send,
+    shots_recv,
+    side_send,
+    side_recv,
+    pair_send,
+    pair_recv,
+    sum_send,
+    sum_recv,
+):
+    d = lax.axis_index("depth")
+    g = lax.axis_index("gx")
+    x = lax.axis_index("gy")
+    cz, bx, _ = slowness.shape
+    nd = speeds.shape[0] // cz
+    nx = 2 * bx
+    part = lax.rem(d, 4)
+    quad = d // 4
+    sibling = {"gx": 1 - g}
+    across = {"gy": 1 - x}
+    mine = pl.ds(pl.multiple_of(bx * g, bx), bx)
+    theirs = pl.ds(pl.multiple_of(bx * (1 - g), bx), bx)
+    shots = pl.ds(4 * quad, 4)
+
+    loads = [
+        pltpu.make_async_copy(source, target, load_sem.at[i])
+        for i, (source, target) in enumerate(
+            (
+                (slowness_hbm, slowness),
+                (air_hbm, air),
+                (reflector_hbm, reflect),
+                (receiver_hbm.at[shots], receiver),
+                (residual_hbm.at[shots], resid),
+            )
+        )
+    ]
+    for load in loads:
+        load.start()
+    barrier = pltpu.get_barrier_semaphore()
+
+    def greet(i, carry):
+        pl.semaphore_signal(barrier, inc=1, device_id={"depth": lax.rem(d + i, nd)}, device_id_type=pl.DeviceIdType.MESH)
+        return carry
+
+    lax.fori_loop(1, nd, greet, 0)
+    for peer in (sibling, across):
+        pl.semaphore_signal(barrier, inc=1, device_id=peer, device_id_type=pl.DeviceIdType.MESH)
+
+    def remote(source, target, send, recv, peer):
+        return pltpu.make_async_remote_copy(
+            src_ref=source,
+            dst_ref=target,
+            send_sem=send,
+            recv_sem=recv,
+            device_id=peer,
+            device_id_type=pl.DeviceIdType.MESH,
+        )
+
+    loads[0].wait()
+    loads[1].wait()
+    speed = jnp.where(air[...] == 1, jnp.float32(AIR_SLOW), slowness[...])
+    first, second = speed[:, :, :WIDE], speed[:, :, WIDE:]
+    rim_out[...] = jnp.where(x == 0, second, first)
+    for p in range(4):
+        wins[p] = part_window(p, x, first, second, first)
+    pl.semaphore_wait(barrier, nd + 1)
+
+    rim = remote(rim_out, rim_in, rim_send, rim_recv, across)
+    rim.start()
+    late = 3 * (1 - x)
+
+    def slab(target):
+        return remote(
+            wins.at[lax.rem(target, 4)],
+            speeds.at[pl.ds(cz * d, cz), mine],
+            slab_send.at[target],
+            slab_recv.at[d],
+            {"depth": target},
+        )
+
+    def send_early(i, carry):
+        target = lax.rem(d + i, nd)
+
+        @pl.when(lax.rem(target, 4) != late)
+        def _():
+            slab(target).start()
+
+        return carry
+
+    lax.fori_loop(1, nd, send_early, 0)
+    for load in loads[2:]:
+        load.wait()
+    source = jnp.where(receiver[...] == 1, resid[...], jnp.float32(0.0))
+    shots_rim_out[0:4] = jnp.where(x == 0, source[:, :, WIDE:], source[:, :, :WIDE])
+    depth_of = reflect[...].astype(jnp.float32)
+    shots_rim_out[4] = jnp.where(x == 0, depth_of[:, WIDE:], depth_of[:, :WIDE])
+    shots_rim = remote(shots_rim_out, shots_rim_in, shots_send, shots_recv, across)
+    shots_rim.start()
+
+    rim.wait_recv()
+    beyond = rim_in[...]
+    wins[late] = jnp.where(
+        x == 0, part_window(3, 0, first, second, beyond), part_window(0, 1, first, second, beyond)
+    )
+    for turn in range(2):
+        target = lax.rem(late + 4 * ((quad + 1 + turn) % 2), nd)
+
+        @pl.when(target != d)
+        def _():
+            slab(target).start()
+
+    speeds[pl.ds(cz * d, cz), mine] = wins[part]
+    stencil_factors(factors, shot_cells_ref, 2 * quad + g, 4 * x + part, nx, ny)
+
+    shots_rim.wait_recv()
+
+    def windowed(first, second, beyond):
+        picks = [part_window(p, x, first, second, beyond) for p in range(4)]
+        return jnp.where(
+            part < 2, jnp.where(part == 0, picks[0], picks[1]), jnp.where(part == 2, picks[2], picks[3])
+        )
+
+    around = windowed(source[:, :, :WIDE], source[:, :, WIDE:], shots_rim_in[0:4])
+    fields[0:2, mine] = jnp.where(g == 0, around[0:2], around[2:4])
+    shots_side[0:2] = jnp.where(g == 0, around[2:4], around[0:2])
+    around = windowed(depth_of[:, :WIDE], depth_of[:, WIDE:], shots_rim_in[4])
+    fields[2, mine] = around
+    shots_side[2] = around
+    side = remote(shots_side, fields.at[:, mine], side_send, side_recv, sibling)
+    side.start()
+
+    def passing(s):
+        block = speeds.at[pl.ds(cz * s, cz), mine]
+        return remote(block, block, pass_send.at[s], pass_recv.at[s], sibling)
+
+    def pass_on(s):
+        @pl.when(s != d)
+        def _():
+            block = speeds.at[pl.ds(cz * s, cz), mine]
+            remote(block, block, slab_send.at[s], slab_recv.at[s], sibling).wait_recv()
+
+        passing(s).start()
+
+    pass_on(0)
+
+    def forward(s, front):
+        @pl.when(s < nd - 1)
+        def _():
+            pass_on(s + 1)
+
+        block = speeds.at[pl.ds(cz * s, cz), theirs]
+        remote(block, block, pass_send.at[s], pass_recv.at[s], sibling).wait_recv()
+        for i in range(2):
+            k = 2 * s + i
+            front = forward_plane(k, speeds[k], front, factors, fronts, spans)
+        return front
+
+    lax.fori_loop(0, nd, forward, jnp.ones((2 * nx, WIDE), jnp.float32))
+    remote(shots_side, fields.at[:, theirs], side_send, side_recv, sibling).wait_recv()
+    source = jnp.concatenate([fields[0], fields[1]], axis=0)
+    reflector = fields[2]
+    shape = (nx, WIDE)
+    col = window_columns(shape, 4 * x + part)
+    row = lax.broadcasted_iota(jnp.int32, shape, 0)
+    lane = lanes(shape)
     inside = (col >= 0) & (col < ny)
-    mine = (lane // OWN) == half
+
+    def pairing(s):
+        return remote(packed.at[s, theirs], sibling_sum.at[s], pair_send.at[s], pair_recv.at[s], sibling)
+
+    def summing(s):
+        return remote(both.at[s], gathered.at[d], sum_send.at[s], sum_recv.at[d], {"depth": s})
+
+    def hand_on(s):
+        pairing(s).wait_recv()
+        total = packed[s, mine] + sibling_sum[s]
+
+        @pl.when(s == d)
+        def _():
+            gathered[s] = total
+
+        @pl.when(s != d)
+        def _():
+            both[s] = total
+            summing(s).start()
 
     def adjoint(step, back):
-        k = nz - 1 - step
-        back, grad = adjoint_plane(
-            k, speed_ref[k], back, source, reflector, factors, fronts, spans, inside, (row == 0, row == nx - 1)
-        )
-        out_ref[k] = jnp.where(mine, grad, 0.0)
+        s = nd - 1 - step
+        grads = []
+        for i in (1, 0):
+            k = 2 * s + i
+            back, grad = adjoint_plane(
+                k, speeds[k], back, source, reflector, factors, fronts, spans, inside, (row == 0, row == nx - 1)
+            )
+            grads.append(grad)
+        packed[s] = jnp.where(lane < OWN, grads[1], halfway(grads[0]))
+        pairing(s).start()
+
+        @pl.when(step > 0)
+        def _():
+            hand_on(s + 1)
+
         return back
 
-    lax.fori_loop(0, nz, adjoint, jnp.zeros((2 * nx, WIDE), jnp.float32))
+    lax.fori_loop(0, nd, adjoint, jnp.zeros((2 * nx, WIDE), jnp.float32))
+    hand_on(0)
+
+    rim.wait_send()
+    shots_rim.wait_send()
+    side.wait_send()
+
+    def finish(s, carry):
+        passing(s).wait_send()
+        pairing(s).wait_send()
+
+        @pl.when(s != d)
+        def _():
+            slab(s).wait_send()
+            summing(s).wait_send()
+            remote(both.at[s], gathered.at[s], sum_send.at[s], sum_recv.at[s], {"depth": s}).wait_recv()
+
+        return carry
+
+    lax.fori_loop(0, nd, finish, 0)
+    totals = [gathered[p] + gathered[4 + p] for p in range(4)]
+    lane = lanes((bx, WIDE))
+    for tile in range(2):
+        low, high = totals[2 * tile], totals[2 * tile + 1]
+        columns = slice(tile * WIDE, (tile + 1) * WIDE)
+        out_ref[0, :, columns] = jnp.where(lane < OWN, low, halfway(high))
+        out_ref[1, :, columns] = jnp.where(lane < OWN, halfway(low), high)
 
 
 def local_split(slowness, air_mask, reflector, shot_cells, receiver_mask, residual):
     cz, bx, by = slowness.shape
-    nz, nx, ny = cz * lax.axis_size("depth"), bx * lax.axis_size("gx"), by * lax.axis_size("gy")
-    depth = lax.axis_index("depth")
-    tile = 2 * lax.axis_index("gy") + lax.rem(depth, 2)
-    half = lax.axis_index("gx")
-    speed = jnp.where(air_mask == 1, jnp.float32(AIR_SLOW), slowness)
-    speed = lax.all_gather(speed, ("depth",), axis=0, tiled=True)
-    source = jnp.where(receiver_mask == 1, residual, jnp.float32(0.0))
-    source = lax.dynamic_slice_in_dim(source, 2 * (depth // 2), 2, axis=0)
-    fields = jnp.concatenate([speed, source, reflector.astype(jnp.float32)[None]], 0)
-    fields = lax.all_gather(lax.all_gather(fields, "gx", axis=1, tiled=True), "gy", axis=2, tiled=True)
-    near = lax.dynamic_slice_in_dim(fields, tile * WIDE, WIDE, axis=2)
-    other = jnp.clip(tile + 2 * half - 1, 0, ny // WIDE - 1)
-    far = lax.dynamic_slice_in_dim(fields, other * WIDE, WIDE, axis=2)
-    lane = jnp.arange(WIDE)
-    own = jnp.where(half == 0, lane < 96, lane >= 32)
-    fields = jnp.where(own, near, far)
-    out = pl.pallas_call(
+    nd = lax.axis_size("depth")
+    nz, nx, ny = cz * nd, bx * lax.axis_size("gx"), by * lax.axis_size("gy")
+    f32, i32 = jnp.float32, jnp.int32
+    dma = pltpu.SemaphoreType.DMA
+    return pl.pallas_call(
         functools.partial(sweep_kernel, ny),
-        out_shape=jax.ShapeDtypeStruct((nz, nx, WIDE), jnp.float32),
-        in_specs=[pl.BlockSpec(memory_space=pltpu.SMEM)] + [pl.BlockSpec(memory_space=pltpu.VMEM)] * 3,
+        out_shape=jax.ShapeDtypeStruct((cz, bx, by), f32),
+        in_specs=[pl.BlockSpec(memory_space=pltpu.SMEM)] + [pl.BlockSpec(memory_space=pl.ANY)] * 5,
         out_specs=pl.BlockSpec(memory_space=pltpu.VMEM),
         scratch_shapes=[
-            pltpu.VMEM((8, 2 * nx, WIDE), jnp.float32),
-            pltpu.VMEM((nz, 2 * nx, WIDE), jnp.float32),
-            pltpu.VMEM((nz, 2 * nx, WIDE), jnp.float32),
+            pltpu.VMEM((cz, bx, by), f32),
+            pltpu.VMEM((cz, bx, by), i32),
+            pltpu.VMEM((bx, by), i32),
+            pltpu.VMEM((4, bx, by), i32),
+            pltpu.VMEM((4, bx, by), f32),
+            pltpu.VMEM((cz, bx, WIDE), f32),
+            pltpu.VMEM((cz, bx, WIDE), f32),
+            pltpu.VMEM((4, cz, bx, WIDE), f32),
+            pltpu.VMEM((nz, nx, WIDE), f32),
+            pltpu.VMEM((5, bx, WIDE), f32),
+            pltpu.VMEM((5, bx, WIDE), f32),
+            pltpu.VMEM((3, bx, WIDE), f32),
+            pltpu.VMEM((3, nx, WIDE), f32),
+            pltpu.VMEM((8, 2 * nx, WIDE), f32),
+            pltpu.VMEM((nz, 2 * nx, WIDE), f32),
+            pltpu.VMEM((nz, 2 * nx, WIDE), f32),
+            pltpu.VMEM((nd, nx, WIDE), f32),
+            pltpu.VMEM((nd, bx, WIDE), f32),
+            pltpu.VMEM((nd, bx, WIDE), f32),
+            pltpu.VMEM((nd, bx, WIDE), f32),
+            dma((5,)),
+            dma,
+            dma,
+            dma((nd,)),
+            dma((nd,)),
+            dma((nd,)),
+            dma((nd,)),
+            dma,
+            dma,
+            dma,
+            dma,
+            dma((nd,)),
+            dma((nd,)),
+            dma((nd,)),
+            dma((nd,)),
         ],
-        compiler_params=pltpu.CompilerParams(vmem_limit_bytes=16 * 1024 * 1024),
-    )(shot_cells, fields[:nz], fields[nz : nz + 2].reshape(2 * nx, WIDE), fields[nz + 2].astype(jnp.int32))
-    zero = jnp.zeros_like(out)
-    first = lax.rem(depth, 2) == 0
-    out = jnp.concatenate([jnp.where(first, out, zero), jnp.where(first, zero, out)], axis=2)
-    out = lax.psum_scatter(out, "depth", scatter_dimension=0, tiled=True)
-    return lax.psum_scatter(out, "gx", scatter_dimension=1, tiled=True)
+        compiler_params=pltpu.CompilerParams(
+            vmem_limit_bytes=16 * 1024 * 1024, collective_id=0, has_side_effects=True
+        ),
+    )(shot_cells, slowness, air_mask, reflector, receiver_mask, residual)
 
 
 def solution(mesh):

time: 153 us -> 34.3 us (0.22)
  waiting for transfers between devices: 95.3 us -> 0 us
  blocking collectives: 34.9 us -> 0 us
  Pallas kernels: 4.4 us -> 28.6 us
  between operations: 13.2 us -> 0.01 us
  local copies, waits for them, and re-layouts: 0.11 us -> 5.41 us
  other arithmetic: 4.34 us -> 0 us
    reduce_scatter x2 -> x0, waiting for transfers between devices: 70.8 us -> none  [the longest x1 62 us: local_split(): out = lax.psum_scatter(out, 'depth', scatter_dimension=0, tiled=True)]
    all_gather x2 -> x0, blocking collectives: 34.9 us -> none  [the longest x1 32.5 us: local_split(): speed = lax.all_gather(speed, ('depth',), axis=0, tiled=True)]
    all_gather x1 -> x0, waiting for transfers between devices: 24.5 us -> none  [local_split(): lax.all_gather(lax.all_gather(fields, 'gx', axis=1, tiled=True), 'gy', ax...]
    pallas_call x1, Pallas kernels: 4.4 us -> 28.6 us  [local_split(): pl.pallas_call(functools.partial(sweep_kernel, ny), out_shape=jax.ShapeDt...]
    unnamed x3 -> x12, local copies, waits for them, and re-layouts: 0.09 us -> 5.41 us
    select_n x5 -> x0, other arithmetic: 2.75 us -> none  [the longest x1 1.13 us: local_split(): fields = jnp.where(own, near, far)]
  transfers between devices with their start and end apart: 3 -> 0, of which waited for: 3 -> 0; matrix products, arithmetic and copies ran while one was open for 0% -> 0% of each run, Pallas kernels for 0% -> 0%
where the time goes in v2:
time: 34.3 us; the launch traced here: 34 us
  Pallas kernels  28.6 us (83%)
  local copies, waits for them, and re-layouts  5.41 us (16%)
    pallas_call x1, Pallas kernels, local_split(): pl.pallas_call(functools.partial(sweep_kernel, ny), out_shape=jax.ShapeDt...  28.6 us
    unnamed x12, local copies, waits for them, and re-layouts  5.41 us

profile of v2, /device:TPU:0, one launch (start us, length us, event | category | flops | bytes accessed | tf_op | source)
XLA Modules:
  0.0 34.0 jit_solution(4538930779712074066)
XLA Ops:
  0.0 0.8 %copy.7.shot_cells_ref = s32[8,2]{1,0:T(8,128)S(1)} copy(s32[8,2]{0,1:T(2,128)} %param.9) | data formatting | bytes 128 | tf_op args[3]
  0.8 0.0 copy-start
  0.8 0.9 %copy-done = s32[8,16,256]{2,1,0:T(8,128)S(1)} copy-done((s32[8,16,256]{2,1,0:T(8,128)S(1)}, s32[8,16,256]{2,1,0:T(8,128)}, u32[]{:S(2)}) %copy-start) | copy-done | bytes 131096
  1.7 0.0 copy-start.1
  1.7 0.9 %copy-done.1 = f32[8,16,256]{2,1,0:T(8,128)S(1)} copy-done((f32[8,16,256]{2,1,0:T(8,128)S(1)}, f32[8,16,256]{2,1,0:T(8,128)}, u32[]{:S(2)}) %copy-start.1) | copy-done | bytes 131096
  2.6 0.0 copy-start.2
  2.6 0.8 %copy-done.2 = f32[2,16,256]{2,1,0:T(8,128)S(1)} copy-done((f32[2,16,256]{2,1,0:T(8,128)S(1)}, f32[2,16,256]{2,1,0:T(8,128)}, u32[]{:S(2)}) %copy-start.2) | copy-done | bytes 32792
  3.3 0.0 copy-start.3
  3.3 0.8 %copy-done.3 = s32[2,16,256]{2,1,0:T(8,128)S(1)} copy-done((s32[2,16,256]{2,1,0:T(8,128)S(1)}, s32[2,16,256]{2,1,0:T(8,128)}, u32[]{:S(2)}) %copy-start.3) | copy-done | bytes 32792
  4.1 0.0 copy-start.4
  4.1 0.7 %copy-done.4 = s32[16,256]{1,0:T(8,128)S(1)} copy-done((s32[16,256]{1,0:T(8,128)S(1)}, s32[16,256]{1,0:T(8,128)}, u32[]{:S(2)}) %copy-start.4) | copy-done | bytes 16408
  4.8 28.6 %shard_map.64 = f32[2,16,256]{2,1,0:T(8,128)S(1)} custom-call(s32[8,2]{1,0:T(8,128)S(1)} %copy.7.shot_cells_ref, f32[2,16,256]{2,1,0:T(8,128)S(1)} %copy-done.2, s32[2,16,256]{2,1,0:T(8,128)S(1)} %copy-done.3, s32[16,256]{1,0:T(8,128)S(1)} %copy-done.4, s32[8,16,256]{2,1,0:T(8,128)S(1)} %copy-done, f32[8,16,256]{2,1,0:T(8,128)S(1)} %copy-done.1), custom_call_target="tpu_custom_call" | custom-call | tf_op jit(solution)/shard_map/pallas_call | solution.py:595
  33.4 0.6 %copy.9 = f32[2,16,256]{2,1,0:T(8,128)} copy(f32[2,16,256]{2,1,0:T(8,128)S(1)} %shard_map.64) | data formatting | bytes 65536
Async XLA Ops:
  0.8 0.9 %copy-start = (s32[8,16,256]{2,1,0:T(8,128)S(1)}, s32[8,16,256]{2,1,0:T(8,128)}, u32[]{:S(2)}) copy-start(s32[8,16,256]{2,1,0:T(8,128)} %receiver_hbm.1) | copy-start | bytes 393220
  1.7 0.9 %copy-start.1 = (f32[8,16,256]{2,1,0:T(8,128)S(1)}, f32[8,16,256]{2,1,0:T(8,128)}, u32[]{:S(2)}) copy-start(f32[8,16,256]{2,1,0:T(8,128)} %residual_hbm.1) | copy-start | bytes 393220
  2.6 0.8 %copy-start.2 = (f32[2,16,256]{2,1,0:T(8,128)S(1)}, f32[2,16,256]{2,1,0:T(8,128)}, u32[]{:S(2)}) copy-start(f32[2,16,256]{2,1,0:T(8,128)} %slowness_hbm.1) | copy-start | bytes 98308
  3.3 0.8 %copy-start.3 = (s32[2,16,256]{2,1,0:T(8,128)S(1)}, s32[2,16,256]{2,1,0:T(8,128)}, u32[]{:S(2)}) copy-start(s32[2,16,256]{2,1,0:T(8,128)} %air_hbm.1) | copy-start | bytes 98308
  4.1 0.7 %copy-start.4 = (s32[16,256]{1,0:T(8,128)S(1)}, s32[16,256]{1,0:T(8,128)}, u32[]{:S(2)}) copy-start(s32[16,256]{1,0:T(8,128)} %reflector_hbm.1) | copy-start | bytes 49156

commit v3 on v2

--- a/solution.py
+++ b/solution.py
@@ -246,7 +246,7 @@
     row = jnp.where(second, row - nx, row)
     col = window_columns(shape, part)
     place = [
-        jnp.where(second, shot_cells_ref[2 * pair + 1, d], shot_cells_ref[2 * pair, d]).astype(
+        jnp.where(second, shot_cells_ref[d, 2 * pair + 1], shot_cells_ref[d, 2 * pair]).astype(
             jnp.float32
         )
         for d in (0, 1)
@@ -320,13 +320,14 @@
 
 def sweep_kernel(
     ny,
-    shot_cells_ref,
+    shot_cells_hbm,
     slowness_hbm,
     air_hbm,
     reflector_hbm,
     receiver_hbm,
     residual_hbm,
     out_ref,
+    shot_cells_ref,
     slowness,
     air,
     reflect,
@@ -386,6 +387,7 @@
                 (reflector_hbm, reflect),
                 (receiver_hbm.at[shots], receiver),
                 (residual_hbm.at[shots], resid),
+                (shot_cells_hbm, shot_cells_ref),
             )
         )
     ]
@@ -428,7 +430,7 @@
         return remote(
             wins.at[lax.rem(target, 4)],
             speeds.at[pl.ds(cz * d, cz), mine],
-            slab_send.at[target],
+            slab_send,
             slab_recv.at[d],
             {"depth": target},
         )
@@ -464,7 +466,12 @@
         def _():
             slab(target).start()
 
+    def passing(s):
+        block = speeds.at[pl.ds(cz * s, cz), mine]
+        return remote(block, block, pass_send, pass_recv.at[s], sibling)
+
     speeds[pl.ds(cz * d, cz), mine] = wins[part]
+    passing(d).start()
     stencil_factors(factors, shot_cells_ref, 2 * quad + g, 4 * x + part, nx, ny)
 
     shots_rim.wait_recv()
@@ -484,17 +491,12 @@
     side = remote(shots_side, fields.at[:, mine], side_send, side_recv, sibling)
     side.start()
 
-    def passing(s):
-        block = speeds.at[pl.ds(cz * s, cz), mine]
-        return remote(block, block, pass_send.at[s], pass_recv.at[s], sibling)
-
     def pass_on(s):
         @pl.when(s != d)
         def _():
             block = speeds.at[pl.ds(cz * s, cz), mine]
-            remote(block, block, slab_send.at[s], slab_recv.at[s], sibling).wait_recv()
-
-        passing(s).start()
+            remote(block, block, slab_send, slab_recv.at[s], sibling).wait_recv()
+            passing(s).start()
 
     pass_on(0)
 
@@ -504,7 +506,7 @@
             pass_on(s + 1)
 
         block = speeds.at[pl.ds(cz * s, cz), theirs]
-        remote(block, block, pass_send.at[s], pass_recv.at[s], sibling).wait_recv()
+        remote(block, block, pass_send, pass_recv.at[s], sibling).wait_recv()
         for i in range(2):
             k = 2 * s + i
             front = forward_plane(k, speeds[k], front, factors, fronts, spans)
@@ -521,10 +523,10 @@
     inside = (col >= 0) & (col < ny)
 
     def pairing(s):
-        return remote(packed.at[s, theirs], sibling_sum.at[s], pair_send.at[s], pair_recv.at[s], sibling)
+        return remote(packed.at[s, theirs], sibling_sum.at[s], pair_send, pair_recv.at[s], sibling)
 
     def summing(s):
-        return remote(both.at[s], gathered.at[d], sum_send.at[s], sum_recv.at[d], {"depth": s})
+        return remote(both.at[s], gathered.at[d], sum_send, sum_recv, {"depth": s})
 
     def hand_on(s):
         pairing(s).wait_recv()
@@ -563,20 +565,14 @@
     rim.wait_send()
     shots_rim.wait_send()
     side.wait_send()
-
-    def finish(s, carry):
-        passing(s).wait_send()
-        pairing(s).wait_send()
-
-        @pl.when(s != d)
-        def _():
-            slab(s).wait_send()
-            summing(s).wait_send()
-            remote(both.at[s], gathered.at[s], sum_send.at[s], sum_recv.at[s], {"depth": s}).wait_recv()
-
-        return carry
-
-    lax.fori_loop(0, nd, finish, 0)
+    others = speeds.at[pl.ds(0, cz * (nd - 1)), mine]
+    remote(others, others, slab_send, rim_recv, sibling).wait_send()
+    block = speeds.at[:, mine]
+    remote(block, block, pass_send, rim_recv, sibling).wait_send()
+    remote(packed.at[:, theirs], sibling_sum, pair_send, rim_recv, sibling).wait_send()
+    block = gathered.at[pl.ds(0, nd - 1)]
+    remote(block, block, rim_send, sum_recv, sibling).wait_recv()
+    remote(block, block, sum_send, rim_recv, sibling).wait_send()
     totals = [gathered[p] + gathered[4 + p] for p in range(4)]
     lane = lanes((bx, WIDE))
     for tile in range(2):
@@ -595,9 +591,10 @@
     return pl.pallas_call(
         functools.partial(sweep_kernel, ny),
         out_shape=jax.ShapeDtypeStruct((cz, bx, by), f32),
-        in_specs=[pl.BlockSpec(memory_space=pltpu.SMEM)] + [pl.BlockSpec(memory_space=pl.ANY)] * 5,
+        in_specs=[pl.BlockSpec(memory_space=pltpu.HBM)] * 6,
         out_specs=pl.BlockSpec(memory_space=pltpu.VMEM),
         scratch_shapes=[
+            pltpu.SMEM(shot_cells.shape[::-1], i32),
             pltpu.VMEM((cz, bx, by), f32),
             pltpu.VMEM((cz, bx, by), i32),
             pltpu.VMEM((bx, by), i32),
@@ -618,26 +615,26 @@
             pltpu.VMEM((nd, bx, WIDE), f32),
             pltpu.VMEM((nd, bx, WIDE), f32),
             pltpu.VMEM((nd, bx, WIDE), f32),
-            dma((5,)),
+            dma((6,)),
+            dma,
             dma,
             dma,
             dma((nd,)),
+            dma,
             dma((nd,)),
+            dma,
+            dma,
+            dma,
+            dma,
+            dma,
             dma((nd,)),
-            dma((nd,)),
-            dma,
-            dma,
-            dma,
-            dma,
-            dma((nd,)),
-            dma((nd,)),
-            dma((nd,)),
-            dma((nd,)),
+            dma,
+            dma,
         ],
         compiler_params=pltpu.CompilerParams(
-            vmem_limit_bytes=16 * 1024 * 1024, collective_id=0, has_side_effects=True
+            vmem_limit_bytes=60 * 1024 * 1024, collective_id=0, has_side_effects=True
         ),
-    )(shot_cells, slowness, air_mask, reflector, receiver_mask, residual)
+    )(shot_cells.T, slowness, air_mask, reflector, receiver_mask, residual)
 
 
 def solution(mesh):

time: 34.3 us -> 29.6 us (0.86)
  local copies, waits for them, and re-layouts: 5.41 us -> 1.38 us
  Pallas kernels: 28.6 us -> 28 us
    unnamed x12 -> x1, local copies, waits for them, and re-layouts: 5.41 us -> 1.38 us
    pallas_call x1, Pallas kernels: 28.6 us -> 28 us  [local_split(): pl.pallas_call(functools.partial(sweep_kernel, ny), out_shape=jax.ShapeDt...]
where the time goes in v3:
time: 29.6 us; the launch traced here: 29.4 us
  Pallas kernels  28 us (95%)
  local copies, waits for them, and re-layouts  1.38 us (5%)
    pallas_call x1, Pallas kernels, local_split(): pl.pallas_call(functools.partial(sweep_kernel, ny), out_shape=jax.ShapeDt...  28 us
    unnamed x1, local copies, waits for them, and re-layouts  1.38 us

profile of v3, /device:TPU:0, one launch (start us, length us, event | category | flops | bytes accessed | tf_op | source)
XLA Modules:
  0.0 29.4 jit_solution(16008237587087542448)
XLA Ops:
  0.0 28.0 %shard_map.64 = f32[2,16,256]{2,1,0:T(8,128)} custom-call(s32[2,8]{1,0:T(2,128)} %bitcast.1, f32[2,16,256]{2,1,0:T(8,128)} %slowness_hbm.1, s32[2,16,256]{2,1,0:T(8,128)} %air_hbm.1, s32[16,256]{1,0:T(8,128)} %reflector_hbm.1, s32[8,16,256]{2,1,0:T(8,128)} %receiver_hbm.1, f32[8,16,256]{2,1,0:T(8,128)} %residual_hbm.1), custom_call_target="tpu_custom_call" | custom-call | tf_op jit(solution)/shard_map/pallas_call | solution.py:591
  28.0 1.4 %copy.8 = f32[2,16,256]{2,1,0:T(8,128)} copy(f32[2,16,256]{2,1,0:T(8,128)} %shard_map.64) | data formatting | bytes 65536

commit v4 on v3

--- a/solution.py
+++ b/solution.py
@@ -345,8 +345,6 @@
     fronts,
     spans,
     packed,
-    sibling_sum,
-    both,
     gathered,
     load_sem,
     rim_send,
@@ -359,8 +357,6 @@
     shots_recv,
     side_send,
     side_recv,
-    pair_send,
-    pair_recv,
     sum_send,
     sum_recv,
 ):
@@ -396,7 +392,9 @@
     barrier = pltpu.get_barrier_semaphore()
 
     def greet(i, carry):
-        pl.semaphore_signal(barrier, inc=1, device_id={"depth": lax.rem(d + i, nd)}, device_id_type=pl.DeviceIdType.MESH)
+        for core in range(2):
+            peer = {"depth": lax.rem(d + i, nd), "gx": core}
+            pl.semaphore_signal(barrier, inc=1, device_id=peer, device_id_type=pl.DeviceIdType.MESH)
         return carry
 
     lax.fori_loop(1, nd, greet, 0)
@@ -420,7 +418,7 @@
     rim_out[...] = jnp.where(x == 0, second, first)
     for p in range(4):
         wins[p] = part_window(p, x, first, second, first)
-    pl.semaphore_wait(barrier, nd + 1)
+    pl.semaphore_wait(barrier, 2 * nd)
 
     rim = remote(rim_out, rim_in, rim_send, rim_recv, across)
     rim.start()
@@ -522,24 +520,9 @@
     lane = lanes(shape)
     inside = (col >= 0) & (col < ny)
 
-    def pairing(s):
-        return remote(packed.at[s, theirs], sibling_sum.at[s], pair_send, pair_recv.at[s], sibling)
-
-    def summing(s):
-        return remote(both.at[s], gathered.at[d], sum_send, sum_recv, {"depth": s})
-
-    def hand_on(s):
-        pairing(s).wait_recv()
-        total = packed[s, mine] + sibling_sum[s]
-
-        @pl.when(s == d)
-        def _():
-            gathered[s] = total
-
-        @pl.when(s != d)
-        def _():
-            both[s] = total
-            summing(s).start()
+    def handing(s, core):
+        rows = pl.ds(bx * core, bx)
+        return remote(packed.at[s, rows], gathered.at[2 * d + g], sum_send, sum_recv, {"depth": s, "gx": core})
 
     def adjoint(step, back):
         s = nd - 1 - step
@@ -551,17 +534,16 @@
             )
             grads.append(grad)
         packed[s] = jnp.where(lane < OWN, grads[1], halfway(grads[0]))
-        pairing(s).start()
-
-        @pl.when(step > 0)
-        def _():
-            hand_on(s + 1)
+        for core in range(2):
+
+            @pl.when((s != d) | (g != core))
+            def _():
+                handing(s, core).start()
 
         return back
 
     lax.fori_loop(0, nd, adjoint, jnp.zeros((2 * nx, WIDE), jnp.float32))
-    hand_on(0)
-
+    gathered[2 * d + g] = packed[d, mine]
     rim.wait_send()
     shots_rim.wait_send()
     side.wait_send()
@@ -569,11 +551,13 @@
     remote(others, others, slab_send, rim_recv, sibling).wait_send()
     block = speeds.at[:, mine]
     remote(block, block, pass_send, rim_recv, sibling).wait_send()
-    remote(packed.at[:, theirs], sibling_sum, pair_send, rim_recv, sibling).wait_send()
-    block = gathered.at[pl.ds(0, nd - 1)]
+    block = gathered.at[pl.ds(0, 2 * nd - 1)]
     remote(block, block, rim_send, sum_recv, sibling).wait_recv()
     remote(block, block, sum_send, rim_recv, sibling).wait_send()
-    totals = [gathered[p] + gathered[4 + p] for p in range(4)]
+    totals = [
+        (gathered[2 * p] + gathered[2 * p + 1]) + (gathered[2 * p + 8] + gathered[2 * p + 9])
+        for p in range(4)
+    ]
     lane = lanes((bx, WIDE))
     for tile in range(2):
         low, high = totals[2 * tile], totals[2 * tile + 1]
@@ -612,9 +596,7 @@
             pltpu.VMEM((nz, 2 * nx, WIDE), f32),
             pltpu.VMEM((nz, 2 * nx, WIDE), f32),
             pltpu.VMEM((nd, nx, WIDE), f32),
-            pltpu.VMEM((nd, bx, WIDE), f32),
-            pltpu.VMEM((nd, bx, WIDE), f32),
-            pltpu.VMEM((nd, bx, WIDE), f32),
+            pltpu.VMEM((2 * nd, bx, WIDE), f32),
             dma((6,)),
             dma,
             dma,
@@ -626,15 +608,18 @@
             dma,
             dma,
             dma,
-            dma,
-            dma((nd,)),
             dma,
             dma,
         ],
         compiler_params=pltpu.CompilerParams(
-            vmem_limit_bytes=60 * 1024 * 1024, collective_id=0, has_side_effects=True
+            vmem_limit_bytes=16 * 1024 * 1024, collective_id=0, has_side_effects=True
         ),
-    )(shot_cells.T, slowness, air_mask, reflector, receiver_mask, residual)
+    )(
+        *(
+            pltpu.with_memory_space_constraint(a, pltpu.HBM)
+            for a in (shot_cells.T, slowness, air_mask, reflector, receiver_mask, residual)
+        )
+    )
 
 
 def solution(mesh):

time: 29.6 us -> 25.3 us (0.85)
  Pallas kernels: 28 us -> 24.5 us
  local copies, waits for them, and re-layouts: 1.38 us -> 0.62 us
    pallas_call x1, Pallas kernels: 28 us -> 24.5 us  [local_split(): pl.pallas_call(functools.partial(sweep_kernel, ny), out_shape=jax.ShapeDt...]
    unnamed x1, local copies, waits for them, and re-layouts: 1.38 us -> 0.62 us
where the time goes in v4:
time: 25.3 us; the launch traced here: 25.1 us
  Pallas kernels  24.5 us (97%)
  local copies, waits for them, and re-layouts  0.62 us (2%)
    pallas_call x1, Pallas kernels, local_split(): pl.pallas_call(functools.partial(sweep_kernel, ny), out_shape=jax.ShapeDt...  24.5 us
    unnamed x1, local copies, waits for them, and re-layouts  0.62 us

profile of v4, /device:TPU:0, one launch (start us, length us, event | category | flops | bytes accessed | tf_op | source)
XLA Modules:
  0.0 25.1 jit_solution(11002946094186357064)
XLA Ops:
  0.0 24.5 %shard_map.64 = f32[2,16,256]{2,1,0:T(8,128)S(1)} custom-call(s32[2,8]{1,0:T(2,128)} %bitcast.1, f32[2,16,256]{2,1,0:T(8,128)} %slowness_hbm.1, s32[2,16,256]{2,1,0:T(8,128)} %air_hbm.1, s32[16,256]{1,0:T(8,128)} %reflector_hbm.1, s32[8,16,256]{2,1,0:T(8,128)} %receiver_hbm.1, f32[8,16,256]{2,1,0:T(8,128)} %residual_hbm.1), custom_call_target="tpu_custom_call" | custom-call | tf_op jit(solution)/shard_map/pallas_call | solution.py:575
  24.5 0.6 %copy.8 = f32[2,16,256]{2,1,0:T(8,128)} copy(f32[2,16,256]{2,1,0:T(8,128)S(1)} %shard_map.64) | data formatting | bytes 65536

commit v5 on v4

--- a/solution.py
+++ b/solution.py
@@ -205,6 +205,7 @@
 
 WIDE = 128
 OWN = 64
+PAD = 8
 SIDE = 32
 ROOT2 = math.sqrt(2.0)
 ROOT3 = math.sqrt(3.0)
@@ -216,14 +217,6 @@
 
 def right(cells):
     return pltpu.roll(cells, cells.shape[1] - 1, axis=1)
-
-
-def above(cells):
-    return pltpu.roll(cells, 1, axis=0)
-
-
-def below(cells):
-    return pltpu.roll(cells, cells.shape[0] - 1, axis=0)
 
 
 def halfway(cells):
@@ -271,13 +264,21 @@
     return jnp.concatenate([cells, cells], axis=0)
 
 
-def forward_plane(k, speed, front, factors, fronts, spans):
+def shifted_rows(buffer, cells, nought):
+    rows = cells.shape[0]
+    buffer[pl.ds(PAD, rows)] = cells
+    return buffer[pl.ds(PAD - 1 + nought, rows)], buffer[pl.ds(PAD + 1 + nought, rows)]
+
+
+def forward_plane(k, speed, front, factors, fronts, spans, buffers, nought):
     w1 = twice(jnp.exp(-speed / SOFTMIN_TEMPER))
     w2 = twice(jnp.exp(-(speed * ROOT2) / SOFTMIN_TEMPER))
     w3 = twice(jnp.exp(-(speed * ROOT3) / SOFTMIN_TEMPER))
     side = factors[0] * left(front) + factors[1] * right(front)
-    edge = side + factors[2] * above(front) + factors[3] * below(front)
-    corner = factors[2] * above(side) + factors[3] * below(side)
+    up, down = shifted_rows(buffers[0], front, nought)
+    edge = side + factors[2] * up + factors[3] * down
+    up, down = shifted_rows(buffers[1], side, nought)
+    corner = factors[2] * up + factors[3] * down
     one, two, three = w1 * front, w2 * edge, w3 * corner
     front = one + two + three
     fronts[k] = front
@@ -285,7 +286,7 @@
     return front
 
 
-def adjoint_plane(k, speed, back, source, reflector, factors, fronts, spans, inside, edges):
+def adjoint_plane(k, speed, back, source, reflector, factors, fronts, spans, inside, edges, buffers, nought):
     w1 = twice(jnp.exp(-speed / SOFTMIN_TEMPER))
     w2 = twice(jnp.exp(-(speed * ROOT2) / SOFTMIN_TEMPER))
     w3 = twice(jnp.exp(-(speed * ROOT3) / SOFTMIN_TEMPER))
@@ -295,14 +296,16 @@
     nx = speed.shape[0]
     raw = jnp.where(inside & (speed != AIR_SLOW), part[:nx] + part[nx:], 0.0)
     line = raw + left(raw) + right(raw)
-    box = line + jnp.where(edges[0], 0.0, above(line)) + jnp.where(edges[1], 0.0, below(line))
+    up, down = shifted_rows(buffers[2], line, nought)
+    box = line + jnp.where(edges[0], 0.0, up) + jnp.where(edges[1], 0.0, down)
     grad = 0.4375 * raw + 0.0625 * box
     two, three = w2 * lam, w3 * lam
     far = two + factors[4] * left(three) + factors[5] * right(three)
+    up, down = shifted_rows(buffers[3], far, nought)
     back = (
         w1 * lam
         + (factors[4] * left(two) + factors[5] * right(two))
-        + (factors[6] * above(far) + factors[7] * below(far))
+        + (factors[6] * up + factors[7] * down)
     )
     return back, grad
 
@@ -346,20 +349,24 @@
     spans,
     packed,
     gathered,
-    load_sem,
-    rim_send,
-    rim_recv,
-    slab_send,
-    slab_recv,
-    pass_send,
-    pass_recv,
-    shots_send,
-    shots_recv,
-    side_send,
-    side_recv,
-    sum_send,
-    sum_recv,
+    *rest,
 ):
+    row_buffers, sems = rest[:8], rest[8:]
+    (
+        load_sem,
+        rim_send,
+        rim_recv,
+        slab_send,
+        slab_recv,
+        pass_send,
+        pass_recv,
+        shots_send,
+        shots_recv,
+        side_send,
+        side_recv,
+        sum_send,
+        sum_recv,
+    ) = sems
     d = lax.axis_index("depth")
     g = lax.axis_index("gx")
     x = lax.axis_index("gy")
@@ -387,17 +394,14 @@
             )
         )
     ]
-    for load in loads:
+    for load in loads[:2]:
         load.start()
     barrier = pltpu.get_barrier_semaphore()
 
-    def greet(i, carry):
+    for i in range(nd - 1, 0, -1):
         for core in range(2):
             peer = {"depth": lax.rem(d + i, nd), "gx": core}
             pl.semaphore_signal(barrier, inc=1, device_id=peer, device_id_type=pl.DeviceIdType.MESH)
-        return carry
-
-    lax.fori_loop(1, nd, greet, 0)
     for peer in (sibling, across):
         pl.semaphore_signal(barrier, inc=1, device_id=peer, device_id_type=pl.DeviceIdType.MESH)
 
@@ -411,6 +415,11 @@
             device_id_type=pl.DeviceIdType.MESH,
         )
 
+    for load in loads[2:]:
+        load.start()
+    nought = g // 2
+    for buffer in row_buffers:
+        buffer[...] = jnp.zeros(buffer.shape, jnp.float32)
     loads[0].wait()
     loads[1].wait()
     speed = jnp.where(air[...] == 1, jnp.float32(AIR_SLOW), slowness[...])
@@ -433,16 +442,13 @@
             {"depth": target},
         )
 
-    def send_early(i, carry):
-        target = lax.rem(d + i, nd)
-
-        @pl.when(lax.rem(target, 4) != late)
-        def _():
-            slab(target).start()
-
-        return carry
-
-    lax.fori_loop(1, nd, send_early, 0)
+    for i in range(1, nd):
+        early = lax.rem(d + i, nd)
+
+        @pl.when(lax.rem(early, 4) != late)
+        def _(early=early):
+            slab(early).start()
+
     for load in loads[2:]:
         load.wait()
     source = jnp.where(receiver[...] == 1, resid[...], jnp.float32(0.0))
@@ -507,7 +513,9 @@
         remote(block, block, pass_send, pass_recv.at[s], sibling).wait_recv()
         for i in range(2):
             k = 2 * s + i
-            front = forward_plane(k, speeds[k], front, factors, fronts, spans)
+            front = forward_plane(
+                k, speeds[k], front, factors, fronts, spans, row_buffers[4 * i : 4 * i + 4], nought
+            )
         return front
 
     lax.fori_loop(0, nd, forward, jnp.ones((2 * nx, WIDE), jnp.float32))
@@ -530,7 +538,8 @@
         for i in (1, 0):
             k = 2 * s + i
             back, grad = adjoint_plane(
-                k, speeds[k], back, source, reflector, factors, fronts, spans, inside, (row == 0, row == nx - 1)
+                k, speeds[k], back, source, reflector, factors, fronts, spans, inside,
+                (row == 0, row == nx - 1), row_buffers[4 * i : 4 * i + 4], nought,
             )
             grads.append(grad)
         packed[s] = jnp.where(lane < OWN, grads[1], halfway(grads[0]))
@@ -597,6 +606,7 @@
             pltpu.VMEM((nz, 2 * nx, WIDE), f32),
             pltpu.VMEM((nd, nx, WIDE), f32),
             pltpu.VMEM((2 * nd, bx, WIDE), f32),
+            *[pltpu.VMEM((2 * nx + 2 * PAD, WIDE), f32) for _ in range(8)],
             dma((6,)),
             dma,
             dma,

time: 25.3 us -> 25.4 us (level)
  no operation moved by 1% of the time
where the time goes in v5:
time: 25.4 us; the launch traced here: 25.2 us
  Pallas kernels  24.6 us (97%)
  local copies, waits for them, and re-layouts  0.62 us (2%)
    pallas_call x1, Pallas kernels, local_split(): pl.pallas_call(functools.partial(sweep_kernel, ny), out_shape=jax.ShapeDt...  24.6 us
    unnamed x1, local copies, waits for them, and re-layouts  0.62 us

profile of v5, /device:TPU:0, one launch (start us, length us, event | category | flops | bytes accessed | tf_op | source)
XLA Modules:
  0.0 25.2 jit_solution(11227770111793902842)
XLA Ops:
  0.0 24.6 %shard_map.64 = f32[2,16,256]{2,1,0:T(8,128)S(1)} custom-call(s32[2,8]{1,0:T(2,128)} %bitcast.1, f32[2,16,256]{2,1,0:T(8,128)} %slowness_hbm.1, s32[2,16,256]{2,1,0:T(8,128)} %air_hbm.1, s32[16,256]{1,0:T(8,128)} %reflector_hbm.1, s32[8,16,256]{2,1,0:T(8,128)} %receiver_hbm.1, f32[8,16,256]{2,1,0:T(8,128)} %residual_hbm.1), custom_call_target="tpu_custom_call" | custom-call | tf_op jit(solution)/shard_map/pallas_call | solution.py:584
  24.6 0.6 %copy.8 = f32[2,16,256]{2,1,0:T(8,128)} copy(f32[2,16,256]{2,1,0:T(8,128)S(1)} %shard_map.64) | data formatting | bytes 65536

commit v6 on v5

--- a/solution.py
+++ b/solution.py
@@ -206,6 +206,7 @@
 WIDE = 128
 OWN = 64
 PAD = 8
+AHEAD = 3
 SIDE = 32
 ROOT2 = math.sqrt(2.0)
 ROOT3 = math.sqrt(3.0)
@@ -502,12 +503,13 @@
             remote(block, block, slab_send, slab_recv.at[s], sibling).wait_recv()
             passing(s).start()
 
-    pass_on(0)
+    for s in range(AHEAD):
+        pass_on(s)
 
     def forward(s, front):
-        @pl.when(s < nd - 1)
+        @pl.when(s < nd - AHEAD)
         def _():
-            pass_on(s + 1)
+            pass_on(s + AHEAD)
 
         block = speeds.at[pl.ds(cz * s, cz), theirs]
         remote(block, block, pass_send, pass_recv.at[s], sibling).wait_recv()

time: 25.4 us -> 23.6 us (0.929)
  Pallas kernels: 24.6 us -> 22.9 us
    pallas_call x1, Pallas kernels: 24.6 us -> 22.9 us  [local_split(): pl.pallas_call(functools.partial(sweep_kernel, ny), out_shape=jax.ShapeDt...]
where the time goes in v6:
time: 23.6 us; the launch traced here: 23.5 us
  Pallas kernels  22.9 us (97%)
  local copies, waits for them, and re-layouts  0.62 us (3%)
    pallas_call x1, Pallas kernels, local_split(): pl.pallas_call(functools.partial(sweep_kernel, ny), out_shape=jax.ShapeDt...  22.9 us
    unnamed x1, local copies, waits for them, and re-layouts  0.62 us

profile of v6, /device:TPU:0, one launch (start us, length us, event | category | flops | bytes accessed | tf_op | source)
XLA Modules:
  0.0 23.5 jit_solution(6843517170919626163)
XLA Ops:
  0.0 22.9 %shard_map.64 = f32[2,16,256]{2,1,0:T(8,128)S(1)} custom-call(s32[2,8]{1,0:T(2,128)} %bitcast.1, f32[2,16,256]{2,1,0:T(8,128)} %slowness_hbm.1, s32[2,16,256]{2,1,0:T(8,128)} %air_hbm.1, s32[16,256]{1,0:T(8,128)} %reflector_hbm.1, s32[8,16,256]{2,1,0:T(8,128)} %receiver_hbm.1, f32[8,16,256]{2,1,0:T(8,128)} %residual_hbm.1), custom_call_target="tpu_custom_call" | custom-call | tf_op jit(solution)/shard_map/pallas_call | solution.py:586
  22.9 0.6 %copy.8 = f32[2,16,256]{2,1,0:T(8,128)} copy(f32[2,16,256]{2,1,0:T(8,128)S(1)} %shard_map.64) | data formatting | bytes 65536

commit v7 on v6

--- a/solution.py
+++ b/solution.py
@@ -479,6 +479,16 @@
     passing(d).start()
     stencil_factors(factors, shot_cells_ref, 2 * quad + g, 4 * x + part, nx, ny)
 
+    def pass_on(s):
+        @pl.when(s != d)
+        def _():
+            block = speeds.at[pl.ds(cz * s, cz), mine]
+            remote(block, block, slab_send, slab_recv.at[s], sibling).wait_recv()
+            passing(s).start()
+
+    for s in range(AHEAD):
+        pass_on(s)
+
     shots_rim.wait_recv()
 
     def windowed(first, second, beyond):
@@ -495,16 +505,6 @@
     shots_side[2] = around
     side = remote(shots_side, fields.at[:, mine], side_send, side_recv, sibling)
     side.start()
-
-    def pass_on(s):
-        @pl.when(s != d)
-        def _():
-            block = speeds.at[pl.ds(cz * s, cz), mine]
-            remote(block, block, slab_send, slab_recv.at[s], sibling).wait_recv()
-            passing(s).start()
-
-    for s in range(AHEAD):
-        pass_on(s)
 
     def forward(s, front):
         @pl.when(s < nd - AHEAD)

time: 23.6 us -> 23.6 us (level)
  no operation moved by 1% of the time
where the time goes in v7:
time: 23.6 us; the launch traced here: 23.5 us
  Pallas kernels  22.9 us (97%)
  local copies, waits for them, and re-layouts  0.62 us (3%)
    pallas_call x1, Pallas kernels, local_split(): pl.pallas_call(functools.partial(sweep_kernel, ny), out_shape=jax.ShapeDt...  22.9 us
    unnamed x1, local copies, waits for them, and re-layouts  0.62 us

profile of v7, /device:TPU:0, one launch (start us, length us, event | category | flops | bytes accessed | tf_op | source)
XLA Modules:
  0.0 23.5 jit_solution(15619053808955053213)
XLA Ops:
  0.0 22.9 %shard_map.64 = f32[2,16,256]{2,1,0:T(8,128)S(1)} custom-call(s32[2,8]{1,0:T(2,128)} %bitcast.1, f32[2,16,256]{2,1,0:T(8,128)} %slowness_hbm.1, s32[2,16,256]{2,1,0:T(8,128)} %air_hbm.1, s32[16,256]{1,0:T(8,128)} %reflector_hbm.1, s32[8,16,256]{2,1,0:T(8,128)} %receiver_hbm.1, f32[8,16,256]{2,1,0:T(8,128)} %residual_hbm.1), custom_call_target="tpu_custom_call" | custom-call | tf_op jit(solution)/shard_map/pallas_call | solution.py:586
  22.9 0.6 %copy.8 = f32[2,16,256]{2,1,0:T(8,128)} copy(f32[2,16,256]{2,1,0:T(8,128)S(1)} %shard_map.64) | data formatting | bytes 65536

commit v8 on v7

--- a/solution.py
+++ b/solution.py
@@ -374,7 +374,12 @@
     cz, bx, _ = slowness.shape
     nd = speeds.shape[0] // cz
     nx = 2 * bx
-    part = lax.rem(d, 4)
+
+    def part_of(depth):
+        place = lax.rem(depth, 4)
+        return place + (1 - x) * (3 - 2 * place)
+
+    part = part_of(d)
     quad = d // 4
     sibling = {"gx": 1 - g}
     across = {"gy": 1 - x}
@@ -436,7 +441,7 @@
 
     def slab(target):
         return remote(
-            wins.at[lax.rem(target, 4)],
+            wins.at[part_of(target)],
             speeds.at[pl.ds(cz * d, cz), mine],
             slab_send,
             slab_recv.at[d],
@@ -446,9 +451,21 @@
     for i in range(1, nd):
         early = lax.rem(d + i, nd)
 
-        @pl.when(lax.rem(early, 4) != late)
+        @pl.when(lax.rem(early, 4) != 0)
         def _(early=early):
             slab(early).start()
+
+    rim.wait_recv()
+    beyond = rim_in[...]
+    wins[late] = jnp.where(
+        x == 0, part_window(3, 0, first, second, beyond), part_window(0, 1, first, second, beyond)
+    )
+    for turn in range(2):
+        target = 4 * ((quad + 1 + turn) % 2)
+
+        @pl.when(target != d)
+        def _():
+            slab(target).start()
 
     for load in loads[2:]:
         load.wait()
@@ -458,18 +475,6 @@
     shots_rim_out[4] = jnp.where(x == 0, depth_of[:, WIDE:], depth_of[:, :WIDE])
     shots_rim = remote(shots_rim_out, shots_rim_in, shots_send, shots_recv, across)
     shots_rim.start()
-
-    rim.wait_recv()
-    beyond = rim_in[...]
-    wins[late] = jnp.where(
-        x == 0, part_window(3, 0, first, second, beyond), part_window(0, 1, first, second, beyond)
-    )
-    for turn in range(2):
-        target = lax.rem(late + 4 * ((quad + 1 + turn) % 2), nd)
-
-        @pl.when(target != d)
-        def _():
-            slab(target).start()
 
     def passing(s):
         block = speeds.at[pl.ds(cz * s, cz), mine]
@@ -569,6 +574,7 @@
         (gathered[2 * p] + gathered[2 * p + 1]) + (gathered[2 * p + 8] + gathered[2 * p + 9])
         for p in range(4)
     ]
+    totals = [jnp.where(x == 0, totals[3 - p], totals[p]) for p in range(4)]
     lane = lanes((bx, WIDE))
     for tile in range(2):
         low, high = totals[2 * tile], totals[2 * tile + 1]

time: 23.6 us -> 21.7 us (0.919)
  Pallas kernels: 22.9 us -> 20.9 us
    pallas_call x1, Pallas kernels: 22.9 us -> 20.9 us  [local_split(): pl.pallas_call(functools.partial(sweep_kernel, ny), out_shape=jax.ShapeDt...]
where the time goes in v8:
time: 21.7 us; the launch traced here: 21.5 us
  Pallas kernels  20.9 us (96%)
  local copies, waits for them, and re-layouts  0.62 us (3%)
    pallas_call x1, Pallas kernels, local_split(): pl.pallas_call(functools.partial(sweep_kernel, ny), out_shape=jax.ShapeDt...  20.9 us
    unnamed x1, local copies, waits for them, and re-layouts  0.62 us

profile of v8, /device:TPU:0, one launch (start us, length us, event | category | flops | bytes accessed | tf_op | source)
XLA Modules:
  0.0 21.5 jit_solution(16111014547297137844)
XLA Ops:
  0.0 20.9 %shard_map.64 = f32[2,16,256]{2,1,0:T(8,128)S(1)} custom-call(s32[2,8]{1,0:T(2,128)} %bitcast.1, f32[2,16,256]{2,1,0:T(8,128)} %slowness_hbm.1, s32[2,16,256]{2,1,0:T(8,128)} %air_hbm.1, s32[16,256]{1,0:T(8,128)} %reflector_hbm.1, s32[8,16,256]{2,1,0:T(8,128)} %receiver_hbm.1, f32[8,16,256]{2,1,0:T(8,128)} %residual_hbm.1), custom_call_target="tpu_custom_call" | custom-call | tf_op jit(solution)/shard_map/pallas_call | solution.py:592
  20.9 0.6 %copy.8 = f32[2,16,256]{2,1,0:T(8,128)} copy(f32[2,16,256]{2,1,0:T(8,128)S(1)} %shard_map.64) | data formatting | bytes 65536

commit v9 on v8

--- a/solution.py
+++ b/solution.py
@@ -206,7 +206,7 @@
 WIDE = 128
 OWN = 64
 PAD = 8
-AHEAD = 3
+AHEAD = 5
 SIDE = 32
 ROOT2 = math.sqrt(2.0)
 ROOT3 = math.sqrt(3.0)

time: 21.7 us -> 21.5 us (level)
  no operation moved by 1% of the time
where the time goes in v9:
time: 21.5 us; the launch traced here: 21.4 us
  Pallas kernels  20.7 us (96%)
  local copies, waits for them, and re-layouts  0.62 us (3%)
    pallas_call x1, Pallas kernels, local_split(): pl.pallas_call(functools.partial(sweep_kernel, ny), out_shape=jax.ShapeDt...  20.7 us
    unnamed x1, local copies, waits for them, and re-layouts  0.62 us

profile of v9, /device:TPU:0, one launch (start us, length us, event | category | flops | bytes accessed | tf_op | source)
XLA Modules:
  0.0 21.4 jit_solution(5166197071881248592)
XLA Ops:
  0.0 20.7 %shard_map.64 = f32[2,16,256]{2,1,0:T(8,128)S(1)} custom-call(s32[2,8]{1,0:T(2,128)} %bitcast.1, f32[2,16,256]{2,1,0:T(8,128)} %slowness_hbm.1, s32[2,16,256]{2,1,0:T(8,128)} %air_hbm.1, s32[16,256]{1,0:T(8,128)} %reflector_hbm.1, s32[8,16,256]{2,1,0:T(8,128)} %receiver_hbm.1, f32[8,16,256]{2,1,0:T(8,128)} %residual_hbm.1), custom_call_target="tpu_custom_call" | custom-call | tf_op jit(solution)/shard_map/pallas_call | solution.py:592
  20.7 0.6 %copy.8 = f32[2,16,256]{2,1,0:T(8,128)} copy(f32[2,16,256]{2,1,0:T(8,128)S(1)} %shard_map.64) | data formatting | bytes 65536
